TPU v7x, 32 devices: a whole 2x2x4 slice. The times are simulated.
32 devices in a mesh: dp: 8 (over z, y), tensor: 4 (over x, core).
Axes of the slice: x: 2, y: 2, z: 4, core: 2. Of those that a mesh axis runs over, the one named last changes fastest.
Arguments:
- layer_input: bfloat16 [2048, 2048], P('dp'), may hold values from -6 to 6
- upstream: bfloat16 [2048, 2048], P('dp'), may hold values from -6 to 6
- norm_gains: float32 [4, 2048], replicated, may hold values from 0.5 to 1.5
- mixer_input: bfloat16 [2048, 2, 4096], P('dp', None, 'tensor'), may hold values from -0.125 to 0.125
- conv_taps: float32 [4, 4096], P(None, 'tensor'), may hold values from -3 to 3
- conv_bias: float32 [4096], P('tensor'), may hold values from -1.8 to 1.8
- mixer_select: bfloat16 [160, 4096], P('dp', 'tensor'), may hold values from -0.09375 to 0.09375
- mixer_step: bfloat16 [128, 4096], P('dp', 'tensor'), may hold values from -0.5 to 0.5
- step_bias: float32 [4096], P('tensor'), may hold values from -6.5 to -2.5
- decay_log: float32 [16, 4096], P(None, 'tensor'), may hold values from 0 to 2.77
- skip_gain: float32 [4096], P('tensor'), may hold values from 0.1 to 1.9
- mixer_output: bfloat16 [2048, 4096], P('dp', 'tensor'), may hold values from -0.09375 to 0.09375
- first_gate_up: bfloat16 [2048, 2, 4096], P('dp', None, 'tensor'), may hold values from -0.125 to 0.125
- first_down: bfloat16 [2048, 4096], P('dp', 'tensor'), may hold values from -0.09375 to 0.09375
- attention_input: bfloat16 [2048, 3, 2048], P('dp', None, 'tensor'), may hold values from -0.125 to 0.125
- attention_output: bfloat16 [2048, 2048], P('dp', 'tensor'), may hold values from -1.5 to 1.5
- second_gate_up: bfloat16 [2048, 2, 4096], P('dp', None, 'tensor'), may hold values from -0.125 to 0.125
- second_down: bfloat16 [2048, 4096], P('dp', 'tensor'), may hold values from -0.09375 to 0.09375
Outputs:
- layer_output: bfloat16 [2048, 2048], P('dp')
- input_gradient: float32 [2048, 2048], P('dp')
- norm_gains_gradient: float32 [4, 2048], replicated
- mixer_input_gradient: float32 [2048, 2, 4096], P('dp', None, 'tensor')
- conv_taps_gradient: float32 [4, 4096], P(None, 'tensor')
- conv_bias_gradient: float32 [4096], P('tensor')
- mixer_select_gradient: float32 [160, 4096], P('dp', 'tensor')
- mixer_step_gradient: float32 [128, 4096], P('dp', 'tensor')
- step_bias_gradient: float32 [4096], P('tensor')
- decay_log_gradient: float32 [16, 4096], P(None, 'tensor')
- skip_gain_gradient: float32 [4096], P('tensor')
- mixer_output_gradient: float32 [2048, 4096], P('dp', 'tensor')
- first_gate_up_gradient: float32 [2048, 2, 4096], P('dp', None, 'tensor')
- first_down_gradient: float32 [2048, 4096], P('dp', 'tensor')
- attention_input_gradient: float32 [2048, 3, 2048], P('dp', None, 'tensor')
- attention_output_gradient: float32 [2048, 2048], P('dp', 'tensor')
- second_gate_up_gradient: float32 [2048, 2, 4096], P('dp', None, 'tensor')
- second_down_gradient: float32 [2048, 4096], P('dp', 'tensor')
All inputs are finite; a program needn't handle non-finite values.
Results may differ from a plain program's by a relative error of at most 0.033.
Values may be sent and summed in bfloat16 or wider, within the bound.
No kernel may reach another device: no remote copies, remote signals or barrier semaphores. Data moves between devices by JAX's collectives and lax.ppermute only.
A program may use at most 256 MiB of HBM per device.

v0:
```python
import functools
import jax
import jax.numpy as jnp
from jax import lax
from jax.experimental import pallas as pl
from jax.experimental.pallas import tpu as pltpu
from jax.sharding import PartitionSpec as P

HEAD_DIM = 64
WINDOW = 2048
EPS = 1e-05
ROPE_BASE = 10000.0
MASKED = -1e30
BF = jnp.bfloat16
F32 = jnp.float32
SWAP = ((0, 1), (1, 0))
QUARTERS = 4
LANES = 128
ROWS = 8


def scan_forward_kernel(
    x_ref, raw_ref, gate_ref, sel_ref, bias_ref, decay_ref, skip_ref, y_ref, gated_ref, hist_ref, state_ref
):
    seqs, steps, channels = x_ref.shape
    blocks = channels // LANES
    states_n = decay_ref.shape[0]
    pairs = [(s, j) for s in range(seqs) for j in range(blocks)]

    @pl.when(pl.program_id(0) == 0)
    def _():
        state_ref[...] = jnp.zeros_like(state_ref)

    def lanes(j):
        return slice(j * LANES, (j + 1) * LANES)

    rates = [-jnp.exp(decay_ref[:, lanes(j)]) for j in range(blocks)]

    def chunk(k, states):
        states = list(states)
        rows = pl.ds(pl.multiple_of(k * ROWS, ROWS), ROWS)
        x_t, d_t, dx_t = {}, {}, {}
        for s, j in pairs:
            x_t[s, j] = x_ref[s, rows, lanes(j)]
            d_t[s, j] = jax.nn.softplus(raw_ref[s, rows, lanes(j)] + bias_ref[:, lanes(j)])
            dx_t[s, j] = d_t[s, j] * x_t[s, j]
        outs = {p: [] for p in pairs}
        for i in range(ROWS):
            for s in range(seqs):
                sel_b = jnp.broadcast_to(sel_ref[s, k, :states_n, i : i + 1], (states_n, LANES))
                sel_c = jnp.broadcast_to(sel_ref[s, k, states_n:, i : i + 1], (states_n, LANES))
                for j in range(blocks):
                    at = s * blocks + j
                    before = states[at]
                    hist_ref[s, k * ROWS + i, :, lanes(j)] = before
                    factor = jnp.exp(d_t[s, j][i : i + 1] * rates[j])
                    after = factor * before + dx_t[s, j][i : i + 1] * sel_b
                    states[at] = after
                    outs[s, j].append(jnp.sum(after * sel_c, axis=0, keepdims=True))
        for s, j in pairs:
            y = jnp.concatenate(outs[s, j], axis=0) + skip_ref[:, lanes(j)] * x_t[s, j]
            gate = gate_ref[s, rows, lanes(j)]
            y_ref[s, rows, lanes(j)] = y
            gated_ref[s, rows, lanes(j)] = y * gate * jax.nn.sigmoid(gate)
        return tuple(states)

    first = tuple(state_ref[s * blocks + j] for s, j in pairs)
    last = lax.fori_loop(0, steps // ROWS, chunk, first)
    for at, value in enumerate(last):
        state_ref[at] = value


def scan_backward_kernel(
    x_ref, raw_ref, gate_ref, y_ref, grad_ref, hist_ref, sel_ref, bias_ref, decay_ref, skip_ref,
    dgate_ref, dx_ref, draw_ref, dsel_ref, ddecay_ref, dskip_ref, dbias_ref, adj_ref,
):
    seqs, steps, channels = x_ref.shape
    blocks = channels // LANES
    states_n = decay_ref.shape[0]
    pairs = [(s, j) for s in range(seqs) for j in range(blocks)]

    @pl.when(pl.program_id(0) == 0)
    def _():
        adj_ref[...] = jnp.zeros_like(adj_ref)
        ddecay_ref[...] = jnp.zeros_like(ddecay_ref)
        dskip_ref[...] = jnp.zeros_like(dskip_ref)
        dbias_ref[...] = jnp.zeros_like(dbias_ref)

    def lanes(j):
        return slice(j * LANES, (j + 1) * LANES)

    rates = [-jnp.exp(decay_ref[:, lanes(j)]) for j in range(blocks)]
    columns = lax.broadcasted_iota(jnp.int32, (states_n, ROWS), 1)

    def chunk(step, carry):
        adjoint, decay_sum = list(carry[0]), list(carry[1])
        k = steps // ROWS - 1 - step
        rows = pl.ds(pl.multiple_of(k * ROWS, ROWS), ROWS)
        x_t, d_t, dx_t, dy_t, z_t = {}, {}, {}, {}, {}
        for s, j in pairs:
            x_t[s, j] = x_ref[s, rows, lanes(j)]
            z_t[s, j] = raw_ref[s, rows, lanes(j)] + bias_ref[:, lanes(j)]
            d_t[s, j] = jax.nn.softplus(z_t[s, j])
            dx_t[s, j] = d_t[s, j] * x_t[s, j]
            gate = gate_ref[s, rows, lanes(j)]
            sig = jax.nn.sigmoid(gate)
            grad = grad_ref[s, rows, lanes(j)]
            dy_t[s, j] = grad * gate * sig
            dgate_ref[s, rows, lanes(j)] = grad * y_ref[s, rows, lanes(j)] * sig * (1.0 + gate * (1.0 - sig))
        first, second = {p: [None] * ROWS for p in pairs}, {p: [None] * ROWS for p in pairs}
        for s in range(seqs):
            db_tile = jnp.zeros((states_n, ROWS), jnp.float32)
            dc_tile = jnp.zeros((states_n, ROWS), jnp.float32)
            for i in reversed(range(ROWS)):
                sel_b = jnp.broadcast_to(sel_ref[s, k, :states_n, i : i + 1], (states_n, LANES))
                sel_c = jnp.broadcast_to(sel_ref[s, k, states_n:, i : i + 1], (states_n, LANES))
                db = jnp.zeros((states_n, LANES), jnp.float32)
                dc = jnp.zeros((states_n, LANES), jnp.float32)
                for j in range(blocks):
                    at = s * blocks + j
                    before = hist_ref[s, k * ROWS + i, :, lanes(j)]
                    delta = d_t[s, j][i : i + 1]
                    drive = dx_t[s, j][i : i + 1]
                    dy = dy_t[s, j][i : i + 1]
                    factor = jnp.exp(delta * rates[j])
                    after = factor * before + drive * sel_b
                    lam = adjoint[at] + dy * sel_c
                    dc = dc + dy * after
                    db = db + drive * lam
                    first[s, j][i] = jnp.sum(lam * sel_b, axis=0, keepdims=True)
                    back = lam * factor
                    adjoint[at] = back
                    through = back * before
                    second[s, j][i] = jnp.sum(rates[j] * through, axis=0, keepdims=True)
                    decay_sum[at] = decay_sum[at] + delta * through
                db_tile = jnp.where(columns == i, jnp.sum(db, axis=1, keepdims=True), db_tile)
                dc_tile = jnp.where(columns == i, jnp.sum(dc, axis=1, keepdims=True), dc_tile)
            dsel_ref[s, k, :states_n, :] = db_tile
            dsel_ref[s, k, states_n:, :] = dc_tile
        for s, j in pairs:
            one = jnp.concatenate(first[s, j], axis=0)
            two = jnp.concatenate(second[s, j], axis=0)
            dx_ref[s, rows, lanes(j)] = dy_t[s, j] * skip_ref[:, lanes(j)] + d_t[s, j] * one
            draw = (two + x_t[s, j] * one) * jax.nn.sigmoid(z_t[s, j])
            draw_ref[s, rows, lanes(j)] = draw
            dskip_ref[:, lanes(j)] += dy_t[s, j] * x_t[s, j]
            dbias_ref[:, lanes(j)] += draw
        return tuple(adjoint), tuple(decay_sum)

    carry = (
        tuple(adj_ref[s * blocks + j] for s, j in pairs),
        tuple(jnp.zeros((states_n, LANES), jnp.float32) for _ in pairs),
    )
    adjoint, decay_sum = lax.fori_loop(0, steps // ROWS, chunk, carry)
    for at, value in enumerate(adjoint):
        adj_ref[at] = value
    for (s, j), value in zip(pairs, decay_sum):
        ddecay_ref[:, lanes(j)] += rates[j] * value


def chunk_steps(length):
    return 32 if length % 32 == 0 else length


def scan_forward(x, raw, gate, sel, bias, decay, skip):
    seqs, length, channels = x.shape
    states_n = decay.shape[0]
    steps = chunk_steps(length)
    act = pl.BlockSpec((seqs, steps, channels), lambda i: (0, i, 0))
    whole = lambda a: pl.BlockSpec(a.shape, lambda i: (0,) * a.ndim)
    vec = lambda v: v.reshape(1, -1)
    elems = seqs * length * channels * states_n
    return pl.pallas_call(
        scan_forward_kernel,
        grid=(length // steps,),
        in_specs=[act, act, act,
            pl.BlockSpec((seqs, steps // ROWS, 2 * states_n, ROWS), lambda i: (0, i, 0, 0)),
            whole(vec(bias)), whole(decay), whole(vec(skip))],
        out_specs=[act, act, pl.BlockSpec((seqs, steps, states_n, channels), lambda i: (0, i, 0, 0))],
        out_shape=[
            jax.ShapeDtypeStruct((seqs, length, channels), jnp.float32),
            jax.ShapeDtypeStruct((seqs, length, channels), jnp.float32),
            jax.ShapeDtypeStruct((seqs, length, states_n, channels), jnp.float32),
        ],
        scratch_shapes=[pltpu.VMEM((seqs * channels // LANES, states_n, LANES), jnp.float32)],
        cost_estimate=pl.CostEstimate(flops=8 * elems, bytes_accessed=4 * elems, transcendentals=elems),
        compiler_params=pltpu.CompilerParams(vmem_limit_bytes=32 * 1024 * 1024),
        name="scan_forward",
    )(x, raw, gate, sel, vec(bias), decay, vec(skip))


def scan_backward(x, raw, gate, y, grad, hist, sel, bias, decay, skip):
    seqs, length, channels = x.shape
    states_n = decay.shape[0]
    steps = chunk_steps(length)
    n = length // steps
    act = pl.BlockSpec((seqs, steps, channels), lambda i: (0, n - 1 - i, 0))
    selspec = pl.BlockSpec((seqs, steps // ROWS, 2 * states_n, ROWS), lambda i: (0, n - 1 - i, 0, 0))
    whole = lambda shape: pl.BlockSpec(shape, lambda i: (0,) * len(shape))
    vec = lambda v: v.reshape(1, -1)
    elems = seqs * length * channels * states_n
    full = jax.ShapeDtypeStruct((seqs, length, channels), jnp.float32)
    return pl.pallas_call(
        scan_backward_kernel,
        grid=(n,),
        in_specs=[act, act, act, act, act,
            pl.BlockSpec((seqs, steps, states_n, channels), lambda i: (0, n - 1 - i, 0, 0)),
            selspec, whole((1, channels)), whole(decay.shape), whole((1, channels))],
        out_specs=[act, act, act, selspec, whole(decay.shape), whole((ROWS, channels)), whole((ROWS, channels))],
        out_shape=[
            full, full, full,
            jax.ShapeDtypeStruct(sel.shape, jnp.float32),
            jax.ShapeDtypeStruct(decay.shape, jnp.float32),
            jax.ShapeDtypeStruct((ROWS, channels), jnp.float32),
            jax.ShapeDtypeStruct((ROWS, channels), jnp.float32),
        ],
        scratch_shapes=[pltpu.VMEM((seqs * channels // LANES, states_n, LANES), jnp.float32)],
        cost_estimate=pl.CostEstimate(flops=20 * elems, bytes_accessed=4 * elems, transcendentals=elems),
        compiler_params=pltpu.CompilerParams(vmem_limit_bytes=32 * 1024 * 1024),
        name="scan_backward",
    )(x, raw, gate, y, grad, hist, sel, vec(bias), decay, vec(skip))


def bit(axis):
    return lax.axis_index(axis)


def exchange(value, axis):
    return lax.ppermute(value, axis, SWAP)


def exchange_diagonal(value):
    return lax.ppermute(value, ("b", "x"), ((0, 3), (1, 2), (2, 1), (3, 0)))


def ordered(axis, mine, other):
    first = bit(axis) == 0
    return lax.select(first, mine, other), lax.select(first, other, mine)


def half_of(value, axis, other=False):
    width = value.shape[-1] // 2
    at = bit(axis) if not other else 1 - bit(axis)
    return lax.dynamic_slice_in_dim(value, at * width, width, axis=value.ndim - 1)


class Layout:
    def __init__(self, high):
        self.high = high
        self.sums = high + ("y",)

    def columns_in(self, value):
        lead = value.shape[:-1]
        k = len(self.high)
        value = value.reshape(lead + (2,) * (k + 2) + (-1,))
        base = len(lead)
        for place, axis in enumerate(self.high + ("b", "y")):
            if axis != "b":
                value = lax.select(bit(axis) == 0, value, lax.rev(value, (base + place,)))
        value = jnp.moveaxis(value, base + k + 1, base)
        return value.reshape(lead + (-1,))

    def columns_out(self, value):
        lead = value.shape[:-1]
        k = len(self.high)
        value = value.reshape(lead + (2,) * (k + 2) + (-1,))
        base = len(lead)
        value = jnp.moveaxis(value, base, base + k + 1)
        for place, axis in enumerate(self.high + ("b", "y")):
            if axis != "b":
                value = lax.select(bit(axis) == 0, value, lax.rev(value, (base + place,)))
        return value.reshape(lead + (-1,))

    def fetch(self, shard):
        mine = half_of(shard, "b")
        other = exchange(half_of(shard, "b", True), "b")
        pieces = [jnp.concatenate(ordered("b", mine, other), axis=0)]
        for axis in self.high[::-1] + ("y",):
            pieces = pieces + [exchange(piece, axis) for piece in pieces]
        return jnp.concatenate(pieces, axis=0)

    def settle(self, grad):
        total = grad
        for axis in ("y",) + self.high:
            rows = total.shape[0] // 2
            total = (total[:rows].astype(F32) + exchange(total[rows:], axis).astype(F32)).astype(BF)
        rows = total.shape[0] // 2
        low, high = total[:rows], total[rows:]
        keep, send = ordered("b", low, high)
        parts = ordered("b", keep, exchange(send, "b"))
        return jnp.concatenate(parts, axis=1).astype(F32)


def gather_rows(rows):
    beside = exchange(rows, "x")
    across = exchange(rows, "b")
    corner = exchange_diagonal(rows)
    mine = jnp.stack([jnp.stack([rows, beside]), jnp.stack([across, corner])])
    other = exchange(mine, "c")
    even, odd = ordered("c", mine, other)
    stacked = jnp.stack([even, odd], axis=2)
    left, right = ordered("x", stacked[:, 0], stacked[:, 1])
    return jnp.stack([left, right], axis=1).reshape(2 * QUARTERS * rows.shape[0], -1)


def gather_sequence(rows):
    even, odd = ordered("c", rows, exchange(rows, "c"))
    pair = jnp.stack([even, odd])
    left, right = ordered("x", pair, exchange(pair, "x"))
    return jnp.stack([left, right]).reshape(QUARTERS * rows.shape[0], -1)


def scatter_rows(partial):
    rows = partial.shape[0] // 8
    value = partial.reshape(2, 2, 2, rows, -1)
    mine = lax.dynamic_index_in_dim(value, bit("c"), 2, False)
    send = lax.dynamic_index_in_dim(value, 1 - bit("c"), 2, False)
    mine = mine + exchange(send.astype(BF), "c").astype(F32)
    here = lax.dynamic_index_in_dim(mine, bit("x"), 1, False)
    there = lax.dynamic_index_in_dim(mine, 1 - bit("x"), 1, False).astype(BF)
    beside = exchange(there[0], "x")
    across = exchange(here[1].astype(BF), "b")
    corner = exchange_diagonal(there[1])
    return here[0] + beside.astype(F32) + across.astype(F32) + corner.astype(F32)


def channel_total(partial):
    total = partial + exchange(partial, "c")
    total = total + exchange(total, "x")
    other = exchange(total, "b")
    rows = total.shape[0] // 2
    return total + jnp.concatenate([other[rows:], other[:rows]], axis=0)


def channel_return(partial):
    total = partial
    for axis in ("c", "x"):
        total = total + exchange(total.astype(BF), axis).astype(F32)
    other = exchange(total.astype(BF), "b").astype(F32)
    rows = total.shape[0] // 2
    return total + jnp.concatenate([other[rows:], other[:rows]], axis=0)


def rms(stream, gain_row):
    scale = lax.rsqrt(jnp.mean(stream * stream, axis=-1, keepdims=True) + EPS)
    return (stream * scale * gain_row[None, :]).astype(BF)


def rms_back(stream, gain_row, grad):
    scale = lax.rsqrt(jnp.mean(stream * stream, axis=-1, keepdims=True) + EPS)
    gain_grad = jnp.sum(grad * stream * scale, axis=0)
    scaled = grad * gain_row[None, :]
    inner = jnp.mean(scaled * stream, axis=-1, keepdims=True)
    return scale * scaled - stream * (scale * scale * scale * inner), gain_grad


def mm(left, right):
    return jnp.dot(left, right, preferred_element_type=F32)


def mm_nt(left, right):
    return lax.dot_general(left, right, (((1,), (1,)), ((), ())), preferred_element_type=F32)


def mm_tn(left, right):
    return lax.dot_general(left, right, (((0,), (0,)), ((), ())), preferred_element_type=F32)


def conv_total(inner, taps, bias):
    count, length = taps.shape[0], inner.shape[1]
    padded = jnp.pad(inner, ((0, 0), (count - 1, 0), (0, 0)))
    total = bias[None, None, :]
    for k in range(count):
        total = total + taps[k][None, None, :] * padded[:, k : k + length]
    return total


def conv_back(grad, inner, taps):
    count, length = taps.shape[0], inner.shape[1]
    before = jnp.pad(inner, ((0, 0), (count - 1, 0), (0, 0)))
    after = jnp.pad(grad, ((0, 0), (0, count - 1), (0, 0)))
    inner_grad = 0.0
    taps_grad = []
    for k in range(count):
        shift = count - 1 - k
        inner_grad = inner_grad + taps[k][None, None, :] * after[:, shift : shift + length]
        taps_grad.append(jnp.sum(grad * before[:, k : k + length], axis=(0, 1)))
    return inner_grad, jnp.stack(taps_grad), jnp.sum(grad, axis=(0, 1))


def mixer_forward(normed, weights, select_weight, step_weight, taps, conv_bias, step_bias, decay_log, skip_gain):
    inner_weight, gate_weight, out_weight = weights
    tokens = normed.shape[0]
    length = tokens // 2
    shaped = lambda v: v.reshape(2, length, -1)
    inner = shaped(mm(normed, inner_weight))
    gate = shaped(mm(normed, gate_weight))
    conv_out = jax.nn.silu(conv_total(inner, taps, conv_bias)).astype(BF)
    flat = conv_out.reshape(tokens, -1)
    selected = channel_total(mm_nt(flat, select_weight))
    rank = step_weight.shape[0]
    step_low = selected[:, :rank].astype(BF)
    raw = shaped(mm(step_low, step_weight))
    sel = selected[:, rank:].reshape(2, length // ROWS, ROWS, -1).transpose(0, 1, 3, 2)
    mixed, gated, hist = scan_forward(conv_out.astype(F32), raw, gate, sel, step_bias, decay_log, skip_gain)
    gated = gated.reshape(tokens, -1).astype(BF)
    partial = mm_nt(gated, out_weight)
    return partial, (normed, inner, gate, conv_out, step_low, raw, sel, mixed, gated, hist)


def mixer_backward(
    stored, low_grad, weights, select_weight, step_weight, taps, conv_bias, step_bias, decay_log, skip_gain
):
    inner_weight, gate_weight, out_weight = weights
    normed, inner, gate, conv_out, step_low, raw, sel, mixed, gated, hist = stored
    tokens = normed.shape[0]
    length = tokens // 2
    shaped = lambda v: v.reshape(2, length, -1)
    flat = lambda v: v.reshape(tokens, -1)
    out_grad = mm_tn(low_grad, gated).astype(BF)
    gated_grad = shaped(mm(low_grad, out_weight))
    gate_grad, conv_scan, raw_grad, sel_grad, decay_grad, skip_grad, bias_grad = scan_backward(
        conv_out.astype(F32), raw, gate, mixed, gated_grad, hist, sel, step_bias, decay_log, skip_gain
    )
    raw_low = flat(raw_grad).astype(BF)
    step_grad = mm_tn(step_low, raw_low)
    step_low_grad = mm_nt(raw_low, step_weight)
    states = sel_grad.transpose(0, 1, 3, 2).reshape(tokens, -1)
    select_low = channel_return(jnp.concatenate([step_low_grad, states], axis=1)).astype(BF)
    select_grad = mm_tn(select_low, flat(conv_out))
    conv_grad = conv_scan + shaped(mm(select_low, select_weight))
    before = conv_total(inner, taps, conv_bias)
    sig = jax.nn.sigmoid(before)
    inner_grad, taps_grad, conv_bias_grad = conv_back(conv_grad * sig * (1.0 + before * (1.0 - sig)), inner, taps)
    inner_low, gate_low = flat(inner_grad.astype(BF)), flat(gate_grad.astype(BF))
    partial = mm_nt(inner_low, inner_weight) + mm_nt(gate_low, gate_weight)
    matrices = (mm_tn(normed, inner_low).astype(BF), mm_tn(normed, gate_low).astype(BF), out_grad)
    small = jnp.concatenate(
        [
            select_grad,
            step_grad,
            taps_grad,
            conv_bias_grad[None],
            jnp.sum(bias_grad, axis=0, keepdims=True),
            decay_grad,
            jnp.sum(skip_grad, axis=0, keepdims=True),
        ],
        axis=0,
    )
    return partial, matrices, small


def ffn_forward(normed, weights):
    gate_weight, up_weight, down_weight = weights
    gate, up = mm(normed, gate_weight), mm(normed, up_weight)
    hidden = (jax.nn.silu(gate) * up).astype(BF)
    return mm_nt(hidden, down_weight), (normed, gate, up, hidden)


def ffn_backward(stored, low_grad, weights):
    gate_weight, up_weight, down_weight = weights
    normed, gate, up, hidden = stored
    hidden_grad = mm(low_grad, down_weight)
    sig = jax.nn.sigmoid(gate)
    gate_low = (hidden_grad * up * sig * (1.0 + gate * (1.0 - sig))).astype(BF)
    up_low = (hidden_grad * gate * sig).astype(BF)
    partial = mm_nt(gate_low, gate_weight) + mm_nt(up_low, up_weight)
    down_grad = mm_tn(low_grad, hidden).astype(BF)
    return partial, (mm_tn(normed, gate_low).astype(BF), mm_tn(normed, up_low).astype(BF), down_grad)


def rotate(values, direction):
    length, size_head = values.shape[1], values.shape[3]
    half_size = size_head // 2
    positions = jnp.arange(length, dtype=F32)
    frequency = ROPE_BASE ** (-jnp.arange(half_size, dtype=F32) * 2.0 / size_head)
    angles = positions[:, None] * frequency[None, :]
    cosine = jnp.cos(angles)[None, :, None, :]
    sine = direction * jnp.sin(angles)[None, :, None, :]
    first, second = values[..., :half_size], values[..., half_size:]
    return jnp.concatenate([first * cosine - second * sine, second * cosine + first * sine], axis=-1)


def masked_scores(queries, keys):
    length = queries.shape[1]
    rows_at = jnp.arange(length)[:, None]
    cols_at = jnp.arange(length)[None, :]
    mask = (cols_at <= rows_at) & (rows_at - cols_at < WINDOW)
    scores = jnp.einsum("sqhd,skhd->shqk", queries, keys, preferred_element_type=F32) * HEAD_DIM**-0.5
    return jnp.where(mask[None, None], scores, MASKED)


def attention_forward(normed, weights):
    in_weight, out_weight = weights
    tokens = normed.shape[0]
    width = in_weight.shape[1] // 3
    triple = mm(normed, in_weight)
    heads = lambda v: v.reshape(2, tokens // 2, width // HEAD_DIM, HEAD_DIM)
    queries = rotate(heads(triple[:, :width]), 1.0).astype(BF)
    keys = rotate(heads(triple[:, width : 2 * width]), 1.0).astype(BF)
    values = heads(triple[:, 2 * width :]).astype(BF)
    scores = masked_scores(queries, keys)
    peak = jnp.max(scores, axis=-1, keepdims=True)
    raised = jnp.exp(scores - peak)
    total = jnp.sum(raised, axis=-1, keepdims=True)
    attend = (raised / total).astype(BF)
    context = jnp.einsum("shqk,skhd->sqhd", attend, values, preferred_element_type=F32)
    context = context.reshape(tokens, width).astype(BF)
    return mm_nt(context, out_weight), (normed, queries, keys, values, peak + jnp.log(total), context)


def attention_backward(stored, low_grad, weights):
    in_weight, out_weight = weights
    normed, queries, keys, values, log_total, context = stored
    tokens = normed.shape[0]
    out_grad = mm_tn(low_grad, context).astype(BF)
    context_grad = mm(low_grad, out_weight).astype(BF).reshape(queries.shape)
    full = jnp.exp(masked_scores(queries, keys) - log_total)
    attend = full.astype(BF)
    value_grad = jnp.einsum("shqk,sqhd->skhd", attend, context_grad, preferred_element_type=F32)
    attend_grad = jnp.einsum("sqhd,skhd->shqk", context_grad, values, preferred_element_type=F32)
    row_delta = jnp.sum(full * attend_grad, axis=-1, keepdims=True)
    score_grad = (full * (attend_grad - row_delta)).astype(BF)
    query_grad = jnp.einsum("shqk,skhd->sqhd", score_grad, keys, preferred_element_type=F32) * HEAD_DIM**-0.5
    key_grad = jnp.einsum("shqk,sqhd->skhd", score_grad, queries, preferred_element_type=F32) * HEAD_DIM**-0.5
    flat = lambda v: v.reshape(tokens, -1)
    triple_low = jnp.concatenate(
        [flat(rotate(query_grad, -1.0)), flat(rotate(key_grad, -1.0)), flat(value_grad)], axis=1
    ).astype(BF)
    return mm_nt(triple_low, in_weight), (mm_tn(normed, triple_low).astype(BF), out_grad)


def shards(
    layout,
    layer_input,
    upstream,
    norm_gains,
    mixer_input,
    conv_taps,
    conv_bias,
    mixer_select,
    mixer_step,
    step_bias,
    decay_log,
    skip_gain,
    mixer_output,
    first_gate_up,
    first_down,
    attention_input,
    attention_output,
    second_gate_up,
    second_down,
):
    mine = lambda v: half_of(v, "b")
    fetch = layout.fetch
    dp_axes = layout.high + ("b", "y")
    quarter = bit("x") * 2 + bit("c")
    rows = layer_input.shape[0] // QUARTERS
    own_rows = lambda v: layout.columns_in(lax.dynamic_slice_in_dim(v, quarter * rows, rows, axis=0))
    gains = layout.columns_in(norm_gains)
    taps, bias_conv, bias_step, decay, skip = (mine(v) for v in (conv_taps, conv_bias, step_bias, decay_log, skip_gain))

    stream0 = own_rows(layer_input).astype(F32)
    normed0 = gather_rows(rms(stream0, gains[0]))
    mixer_weights = (fetch(mixer_input[:, 0]), fetch(mixer_input[:, 1]), fetch(mixer_output))
    select_weight = mine(lax.all_gather(mixer_select, dp_axes, axis=0, tiled=True))
    step_weight = mine(lax.all_gather(mixer_step, dp_axes, axis=0, tiled=True))
    channel = (taps, bias_conv, bias_step, decay, skip)
    partial, mixer_stored = mixer_forward(normed0, mixer_weights, select_weight, step_weight, *channel)
    stream1 = stream0 + scatter_rows(partial)

    first_weights = (fetch(first_gate_up[:, 0]), fetch(first_gate_up[:, 1]), fetch(first_down))
    partial, first_stored = ffn_forward(gather_rows(rms(stream1, gains[1])), first_weights)
    stream2 = stream1 + scatter_rows(partial)

    rows_here = attention_input.shape[0]
    half = attention_input.shape[2] // 2
    triple = attention_input.reshape(rows_here, 3, 2, half).transpose(0, 2, 1, 3).reshape(rows_here, -1)
    attention_weights = (fetch(triple), fetch(attention_output))
    partial, attention_stored = attention_forward(gather_rows(rms(stream2, gains[2])), attention_weights)
    stream3 = stream2 + scatter_rows(partial)

    second_weights = (fetch(second_gate_up[:, 0]), fetch(second_gate_up[:, 1]), fetch(second_down))
    partial, second_stored = ffn_forward(gather_rows(rms(stream3, gains[3])), second_weights)
    stream4 = stream3 + scatter_rows(partial)
    layer_output = gather_sequence(layout.columns_out(stream4.astype(BF)))

    upstream_rows = own_rows(upstream)
    grad4 = upstream_rows.astype(F32)
    partial, second_grads = ffn_backward(second_stored, gather_rows(upstream_rows), second_weights)
    back, gain3 = rms_back(stream3, gains[3], scatter_rows(partial))
    grad3 = grad4 + back
    partial, attention_grads = attention_backward(attention_stored, gather_rows(grad3.astype(BF)), attention_weights)
    back, gain2 = rms_back(stream2, gains[2], scatter_rows(partial))
    grad2 = grad3 + back
    partial, first_grads = ffn_backward(first_stored, gather_rows(grad2.astype(BF)), first_weights)
    back, gain1 = rms_back(stream1, gains[1], scatter_rows(partial))
    grad1 = grad2 + back
    partial, mixer_grads, small = mixer_backward(
        mixer_stored, gather_rows(grad1.astype(BF)), mixer_weights, select_weight, step_weight, *channel
    )
    back, gain0 = rms_back(stream0, gains[0], scatter_rows(partial))
    input_grad = gather_sequence(layout.columns_out(grad1 + back))

    settle = layout.settle
    second_out = [settle(g) for g in second_grads]
    attention_out = [settle(g) for g in attention_grads]
    first_out = [settle(g) for g in first_grads]
    mixer_out = [settle(g) for g in mixer_grads]
    pair = lambda parts: jnp.stack(parts, axis=1)

    for axis in layout.sums:
        small = small + exchange(small.astype(BF), axis).astype(F32)
    small = jnp.concatenate(ordered("b", small, exchange(small.astype(BF), "b").astype(F32)), axis=1)
    dp_index = lax.axis_index(dp_axes)
    select_rows, step_rows = mixer_select.shape[0], mixer_step.shape[0]
    select_all, step_all = select_weight.shape[0], step_weight.shape[0]
    select_grad = lax.dynamic_slice_in_dim(small[:select_all], dp_index * select_rows, select_rows, axis=0)
    step_grad = lax.dynamic_slice_in_dim(
        small[select_all : select_all + step_all], dp_index * step_rows, step_rows, axis=0
    )
    rest = small[select_all + step_all :]
    count, states_n = conv_taps.shape[0], decay_log.shape[0]
    taps_grad, conv_bias_grad, step_bias_grad = rest[:count], rest[count], rest[count + 1]
    decay_grad, skip_grad = rest[count + 2 : count + 2 + states_n], rest[count + 2 + states_n]

    gains_grad = layout.columns_out(jnp.stack([gain0, gain1, gain2, gain3]))
    for axis in ("c", "x", "b", "y") + layout.high:
        gains_grad = gains_grad + exchange(gains_grad, axis)

    triple_grad = attention_out[0].reshape(rows_here, 2, 3, half).transpose(0, 2, 1, 3).reshape(attention_input.shape)
    return (
        layer_output,
        input_grad,
        gains_grad,
        pair(mixer_out[:2]),
        taps_grad,
        conv_bias_grad,
        select_grad,
        step_grad,
        step_bias_grad,
        decay_grad,
        skip_grad,
        mixer_out[2],
        pair(first_out[:2]),
        first_out[2],
        triple_grad,
        attention_out[1],
        pair(second_out[:2]),
        second_out[2],
    )


def solution(mesh):
    n_dp, n_tensor = mesh.devices.shape
    bits = n_dp.bit_length() - 1
    assert n_dp == 1 << bits and bits >= 2 and n_tensor == 4
    high = tuple("a%d" % k for k in range(bits - 2))
    names = high + ("b", "y", "x", "c")
    cube = jax.sharding.Mesh(mesh.devices.reshape((2,) * len(names)), names)
    dp, tensor = high + ("b", "y"), ("x", "c")
    row, both, col = P(dp, None), P(dp, tensor), P(None, tensor)
    three, vec = P(dp, None, tensor), P(tensor)
    return jax.shard_map(
        functools.partial(shards, Layout(high)),
        mesh=cube,
        in_specs=(
            row, row, P(), three, col, vec, both, both, vec, col, vec, both, three, both, three, both, three, both,
        ),
        out_specs=(
            row, row, P(), three, col, vec, both, both, vec, col, vec, both, three, both, three, both, three, both,
        ),
        check_vma=False,
    )
```

profile of v0, /device:TPU:0, one launch (start us, length us, event | category | flops | bytes accessed | tf_op | source)
XLA Modules:
  0.0 1207.9 jit_solution(17013896061706885548)
XLA Ops:
  29.8 33.9 %all-gather = bf16[8,20,1024]{2,1,0:T(8,128)(2,1)} all-gather(bf16[1,20,1024]{2,1,0:T(8,128)(2,1)S(1)} %bitcast.712), channel_id=1, replica_groups=mesh['a0'=2,'b'=2,'y'=2,'x'=2,'c'=2] {'a0','b','y'}, dimensions={0}, use_global_device_ids=true | all-gather | bytes 368640 | tf_op jit(solution)/shard_map/all_gather | solution.py:566
  63.8 33.0 %all_gather.7 = bf16[128,1024]{1,0:T(8,128)(2,1)} all-gather(bf16[16,1024]{1,0:T(8,128)(2,1)S(1)} %copy-done.168), channel_id=1, replica_groups=mesh['a0'=2,'b'=2,'y'=2,'x'=2,'c'=2] {'a0','b','y'}, dimensions={0}, use_global_device_ids=true | all-gather | bytes 294912 | tf_op jit(solution)/shard_map/all_gather | solution.py:567
  142.2 13.8 %collective-permute-done.4 = bf16[256,512]{1,0:T(8,128)(2,1)S(1)} collective-permute-done((bf16[256,512]{1,0:T(8,128)(2,1)S(1)}, bf16[256,512]{1,0:T(8,128)(2,1)S(1)}, u32[]{:S(2)}, u32[]{:S(2)}) %collective-permute-start.4) | collective-permute-done | bytes 262176 | tf_op jit(solution)/shard_map/ppermute | solution.py:229
  182.0 23.2 %collective-permute-start.13 = (bf16[512,512]{1,0:T(8,128)(2,1)S(1)}, bf16[512,512]{1,0:T(8,128)(2,1)S(1)}, u32[]{:S(2)}, u32[]{:S(2)}) collective-permute-start(bf16[512,512]{1,0:T(8,128)(2,1)S(1)} %pad_maximum_fusion.29), channel_id=1, source_target_pairs={{0,4},{4,0},{1,5},{5,1},{2,6},{6,2},{3,7},{7,3},{8,12},{12,8},{9,1... | collective-permute-start | bytes 1572872 | tf_op jit(solution)/shard_map/ppermute | solution.py:229
  256.6 12.2 %collective-permute-done.10 = f32[512,160]{0,1:T(8,128)S(1)} collective-permute-done((f32[512,160]{0,1:T(8,128)S(1)}, f32[512,160]{0,1:T(8,128)S(1)}, u32[]{:S(2)}, u32[]{:S(2)}) %collective-permute-start.10) | collective-permute-done | bytes 327712 | tf_op jit(solution)/shard_map/ppermute | solution.py:229
  272.5 11.1 scan_forward.1
  331.1 21.7 %collective-permute-done.28 = bf16[512,512]{1,0:T(8,128)(2,1)S(1)} collective-permute-done((bf16[512,512]{1,0:T(8,128)(2,1)S(1)}, bf16[512,512]{1,0:T(8,128)(2,1)S(1)}, u32[]{:S(2)}, u32[]{:S(2)}) %collective-permute-start.28) | collective-permute-done | bytes 524320 | tf_op jit(solution)/shard_map/ppermute | solution.py:229
  366.2 11.2 collective-permute-done.30
  436.1 35.1 %collective-permute-done.48 = bf16[512,768]{0,1:T(8,128)(2,1)S(1)} collective-permute-done((bf16[512,768]{0,1:T(8,128)(2,1)S(1)}, bf16[512,768]{0,1:T(8,128)(2,1)S(1)}, u32[]{:S(2)}, u32[]{:S(2)}) %collective-permute-start.48) | collective-permute-done | bytes 786464 | tf_op jit(solution)/shard_map/ppermute | solution.py:229
  476.2 14.3 %collective-permute-done.68 = bf16[512,512]{1,0:T(8,128)(2,1)S(1)} collective-permute-done((bf16[512,512]{1,0:T(8,128)(2,1)}, bf16[512,512]{1,0:T(8,128)(2,1)S(1)}, u32[]{:S(2)}, u32[]{:S(2)}) %collective-permute-start.68) | collective-permute-done | bytes 524320 | tf_op jit(solution)/shard_map/ppermute | solution.py:229
  603.6 14.6 %collective-permute-done.156 = bf16[1024,512]{1,0:T(8,128)(2,1)S(1)} collective-permute-done((bf16[1024,512]{1,0:T(8,128)(2,1)S(1)}, bf16[1024,512]{1,0:T(8,128)(2,1)S(1)}, u32[]{:S(2)}, u32[]{:S(2)}) %collective-permute-start.156) | collective-permute-done | bytes 1048608 | tf_op jit(solution)/shard_map/ppermute | solution.py:229
  620.3 20.5 %collective-permute-done.150 = bf16[1024,512]{1,0:T(8,128)(2,1)S(1)} collective-permute-done((bf16[1024,512]{1,0:T(8,128)(2,1)S(1)}, bf16[1024,512]{1,0:T(8,128)(2,1)S(1)}, u32[]{:S(2)}, u32[]{:S(2)}) %collective-permute-start.150) | collective-permute-done | bytes 1048608 | tf_op jit(solution)/shard_map/ppermute | solution.py:229
  646.2 11.5 collective-permute-done.153
  689.4 10.8 collective-permute-done.152
  791.4 10.8 collective-permute-done.80
  803.4 20.2 %collective-permute-done.145 = bf16[512,768]{0,1:T(8,128)(2,1)S(1)} collective-permute-done((bf16[512,768]{0,1:T(8,128)(2,1)S(1)}, bf16[512,768]{0,1:T(8,128)(2,1)S(1)}, u32[]{:S(2)}, u32[]{:S(2)}) %collective-permute-start.145) | collective-permute-done | bytes 786464 | tf_op jit(solution)/shard_map/ppermute | solution.py:229
  860.9 16.4 %collective-permute-done.135 = bf16[1024,512]{1,0:T(8,128)(2,1)} collective-permute-done((bf16[1024,512]{1,0:T(8,128)(2,1)}, bf16[1024,512]{1,0:T(8,128)(2,1)}, u32[]{:S(2)}, u32[]{:S(2)}) %collective-permute-start.135) | collective-permute-done | bytes 1048608 | tf_op jit(solution)/shard_map/ppermute | solution.py:229
  886.4 12.1 %collective-permute-done.138 = bf16[1024,512]{1,0:T(8,128)(2,1)} collective-permute-done((bf16[1024,512]{1,0:T(8,128)(2,1)}, bf16[1024,512]{1,0:T(8,128)(2,1)}, u32[]{:S(2)}, u32[]{:S(2)}) %collective-permute-start.138) | collective-permute-done | bytes 1048608 | tf_op jit(solution)/shard_map/ppermute | solution.py:229
  966.1 46.0 %scan_backward.1 = (f32[2,256,512]{2,1,0:T(8,128)S(1)}, f32[2,256,512]{2,1,0:T(8,128)S(1)}, f32[2,256,512]{2,1,0:T(8,128)S(1)}, f32[2,32,32,8]{3,2,1,0:T(8,128)S...) custom-call(f32[2,256,512]{2,1,0:T(8,128)S(1)} %get-tuple-element.178.x_ref, ...), custom_call_target="tpu_custom_call" | custom-call | flops 83886080 | bytes 16777216 | tf_op jit(solution)/shard_map/scan_backward/pallas_call | solution.py:203
  1044.4 12.1 collective-permute-done.129
  1059.1 23.7 %collective-permute-done.130 = bf16[311,512]{1,0:T(8,128)(2,1)S(1)} collective-permute-done((bf16[311,512]{1,0:T(8,128)(2,1)S(1)}, bf16[311,512]{1,0:T(8,128)(2,1)S(1)}, u32[]{:S(2)}, u32[]{:S(2)}) %collective-permute-start.130) | collective-permute-done | bytes 318496 | tf_op jit(solution)/shard_map/ppermute | solution.py:229
  1105.6 28.7 %collective-permute-done.133 = bf16[512,512]{1,0:T(8,128)(2,1)S(1)} collective-permute-done((bf16[512,512]{1,0:T(8,128)(2,1)S(1)}, bf16[512,512]{1,0:T(8,128)(2,1)S(1)}, u32[]{:S(2)}, u32[]{:S(2)}) %collective-permute-start.133) | collective-permute-done | bytes 524320 | tf_op jit(solution)/shard_map/ppermute | solution.py:229
  1137.3 23.6 %collective-permute-done.114 = bf16[64,2048]{1,0:T(8,128)(2,1)S(1)} collective-permute-done((bf16[64,2048]{1,0:T(8,128)(2,1)S(1)}, bf16[64,2048]{1,0:T(8,128)(2,1)S(1)}, u32[]{:S(2)}, u32[]{:S(2)}) %collective-permute-start.114) | collective-permute-done | bytes 262176 | tf_op jit(solution)/shard_map/ppermute | solution.py:229
  1194.4 11.4 collective-permute-done.117
  (1168 shorter events, 730.1 us)
Async XLA Ops:
  7.3 122.0 %collective-permute-start.1 = (bf16[64,2048]{1,0:T(8,128)(2,1)}, bf16[64,2048]{1,0:T(8,128)(2,1)}, u32[]{:S(2)}, u32[]{:S(2)}) collective-permute-start(bf16[64,2048]{1,0:T(8,128)(2,1)} %multiply_convert_fusion.11), channel_id=1, source_target_pairs={{0,8},{8,0},{1,9},{9,1},{2,10},{10,2},{3,11},{11,3},{4,12},{12,4},... | collective-permute-start | bytes 786440 | tf_op jit(solution)/shard_map/ppermute | solution.py:229
  10.4 121.9 %collective-permute-start.2 = (bf16[64,2048]{1,0:T(8,128)(2,1)}, bf16[64,2048]{1,0:T(8,128)(2,1)}, u32[]{:S(2)}, u32[]{:S(2)}) collective-permute-start(bf16[64,2048]{1,0:T(8,128)(2,1)} %multiply_convert_fusion.11), channel_id=1, source_target_pairs={{0,10},{2,8},{8,2},{10,0},{1,11},{3,9},{9,3},{11,1},{4,14},{6,12},... | collective-permute-start | bytes 786440 | tf_op jit(solution)/shard_map/ppermute | solution.py:233
  11.7 121.8 %collective-permute-start = (bf16[64,2048]{1,0:T(8,128)(2,1)}, bf16[64,2048]{1,0:T(8,128)(2,1)}, u32[]{:S(2)}, u32[]{:S(2)}) collective-permute-start(bf16[64,2048]{1,0:T(8,128)(2,1)} %multiply_convert_fusion.11), channel_id=1, source_target_pairs={{0,2},{2,0},{1,3},{3,1},{4,6},{6,4},{5,7},{7,5},{8,10},{10,8},{9,1... | collective-permute-start | bytes 786440 | tf_op jit(solution)/shard_map/ppermute | solution.py:229
  12.5 113.8 %collective-permute-start.51 = (bf16[256,256]{1,0:T(8,128)(2,1)}, bf16[256,256]{1,0:T(8,128)(2,1)}, u32[]{:S(2)}, u32[]{:S(2)}) collective-permute-start(bf16[256,256]{1,0:T(8,128)(2,1)} %constant_dynamic-slice_fusion.7), channel_id=1, source_target_pairs={{0,8},{8,0},{1,9},{9,1},{2,10},{10,2},{3,11},{11,3},{4,12},{12,4},... | collective-permute-start | bytes 393224 | tf_op jit(solution)/shard_map/ppermute | solution.py:229
  17.3 158.2 %collective-permute-start.82 = (bf16[64,2048]{1,0:T(8,128)(2,1)S(1)}, bf16[64,2048]{1,0:T(8,128)(2,1)}, u32[]{:S(2)}, u32[]{:S(2)}) collective-permute-start(bf16[64,2048]{1,0:T(8,128)(2,1)S(1)} %reshape.769), channel_id=1, source_target_pairs={{0,8},{8,0},{1,9},{9,1},{2,10},{10,2},{3,11},{11,3},{4,12},{12,4},... | collective-permute-start | bytes 786440 | tf_op jit(solution)/shard_map/ppermute | solution.py:229
  173.6 52.5 %collective-permute-start.3 = (bf16[2,2,64,2048]{3,2,1,0:T(8,128)(2,1)S(1)}, bf16[2,2,64,2048]{3,2,1,0:T(8,128)(2,1)S(1)}, u32[]{:S(2)}, u32[]{:S(2)}) collective-permute-start(bf16[2,2,64,2048]{3,2,1,0:T(8,128)(2,1)S(1)} %pad_maximum_fusion.17), channel_id=1, source_target_pairs={{0,1},{1,0},{2,3},{3,2},{4,5},{5,4},{6,7},{7,6},{8,9},{9,8},{10,11... | collective-permute-start | bytes 3145736 | tf_op jit(solution)/shard_map/ppermute | solution.py:229
  182.0 54.2 %collective-permute-start.13 = (bf16[512,512]{1,0:T(8,128)(2,1)S(1)}, bf16[512,512]{1,0:T(8,128)(2,1)S(1)}, u32[]{:S(2)}, u32[]{:S(2)}) collective-permute-start(bf16[512,512]{1,0:T(8,128)(2,1)S(1)} %pad_maximum_fusion.29), channel_id=1, source_target_pairs={{0,4},{4,0},{1,5},{5,1},{2,6},{6,2},{3,7},{7,3},{8,12},{12,8},{9,1... | collective-permute-start | bytes 1572872 | tf_op jit(solution)/shard_map/ppermute | solution.py:229
  251.7 75.7 %collective-permute-start.32 = (bf16[512,512]{1,0:T(8,128)(2,1)}, bf16[512,512]{1,0:T(8,128)(2,1)}, u32[]{:S(2)}, u32[]{:S(2)}) collective-permute-start(bf16[512,512]{1,0:T(8,128)(2,1)} %pad_maximum_fusion.32), channel_id=1, source_target_pairs={{0,16},{16,0},{1,17},{17,1},{2,18},{18,2},{3,19},{19,3},{4,20},{20... | collective-permute-start | bytes 1572872 | tf_op jit(solution)/shard_map/ppermute | solution.py:229
  330.0 58.2 %collective-permute-start.26 = (bf16[2,2,64,2048]{3,2,1,0:T(8,128)(2,1)S(1)}, bf16[2,2,64,2048]{3,2,1,0:T(8,128)(2,1)S(1)}, u32[]{:S(2)}, u32[]{:S(2)}) collective-permute-start(bf16[2,2,64,2048]{3,2,1,0:T(8,128)(2,1)S(1)} %pad_maximum_fusion.18), channel_id=1, source_target_pairs={{0,1},{1,0},{2,3},{3,2},{4,5},{5,4},{6,7},{7,6},{8,9},{9,8},{10,11... | collective-permute-start | bytes 3145736 | tf_op jit(solution)/shard_map/ppermute | solution.py:229
  377.4 55.8 %collective-permute-start.52 = (bf16[512,256]{1,0:T(8,128)(2,1)S(1)}, bf16[512,256]{1,0:T(8,128)(2,1)S(1)}, u32[]{:S(2)}, u32[]{:S(2)}) collective-permute-start(bf16[512,256]{1,0:T(8,128)(2,1)S(1)} %copy-done.158), channel_id=1, source_target_pairs={{0,16},{16,0},{1,17},{17,1},{2,18},{18,2},{3,19},{19,3},{4,20},{20... | collective-permute-start | bytes 786440 | tf_op jit(solution)/shard_map/ppermute | solution.py:229
  427.8 62.7 %collective-permute-start.68 = (bf16[512,512]{1,0:T(8,128)(2,1)}, bf16[512,512]{1,0:T(8,128)(2,1)S(1)}, u32[]{:S(2)}, u32[]{:S(2)}) collective-permute-start(bf16[512,512]{1,0:T(8,128)(2,1)} %pad_maximum_fusion.35), channel_id=1, source_target_pairs={{0,16},{16,0},{1,17},{17,1},{2,18},{18,2},{3,19},{19,3},{4,20},{20... | collective-permute-start | bytes 1572872 | tf_op jit(solution)/shard_map/ppermute | solution.py:229
  433.0 57.7 %collective-permute-start.49 = (bf16[512,768]{0,1:T(8,128)(2,1)S(1)}, bf16[512,768]{0,1:T(8,128)(2,1)S(1)}, u32[]{:S(2)}, u32[]{:S(2)}) collective-permute-start(bf16[512,768]{0,1:T(8,128)(2,1)S(1)} %pad_maximum_fusion.27), channel_id=1, source_target_pairs={{0,4},{4,0},{1,5},{5,1},{2,6},{6,2},{3,7},{7,3},{8,12},{12,8},{9,1... | collective-permute-start | bytes 2359304 | tf_op jit(solution)/shard_map/ppermute | solution.py:229
  433.1 58.8 %collective-permute-start.46 = (bf16[2,2,64,2048]{3,2,1,0:T(8,128)(2,1)S(1)}, bf16[2,2,64,2048]{3,2,1,0:T(8,128)(2,1)S(1)}, u32[]{:S(2)}, u32[]{:S(2)}) collective-permute-start(bf16[2,2,64,2048]{3,2,1,0:T(8,128)(2,1)S(1)} %pad_maximum_fusion.19), channel_id=1, source_target_pairs={{0,1},{1,0},{2,3},{3,2},{4,5},{5,4},{6,7},{7,6},{8,9},{9,8},{10,11... | collective-permute-start | bytes 3145736 | tf_op jit(solution)/shard_map/ppermute | solution.py:229
  473.5 61.7 %collective-permute-start.69 = (bf16[512,512]{1,0:T(8,128)(2,1)}, bf16[512,512]{1,0:T(8,128)(2,1)}, u32[]{:S(2)}, u32[]{:S(2)}) collective-permute-start(bf16[512,512]{1,0:T(8,128)(2,1)} %pad_maximum_fusion.35), channel_id=1, source_target_pairs={{0,4},{4,0},{1,5},{5,1},{2,6},{6,2},{3,7},{7,3},{8,12},{12,8},{9,1... | collective-permute-start | bytes 1572872 | tf_op jit(solution)/shard_map/ppermute | solution.py:229
  491.3 59.0 %collective-permute-start.84 = (bf16[2,2,64,2048]{3,2,1,0:T(8,128)(2,1)}, bf16[2,2,64,2048]{3,2,1,0:T(8,128)(2,1)}, u32[]{:S(2)}, u32[]{:S(2)}) collective-permute-start(bf16[2,2,64,2048]{3,2,1,0:T(8,128)(2,1)} %pad_maximum_fusion.22), channel_id=1, source_target_pairs={{0,1},{1,0},{2,3},{3,2},{4,5},{5,4},{6,7},{7,6},{8,9},{9,8},{10,11... | collective-permute-start | bytes 3145736 | tf_op jit(solution)/shard_map/ppermute | solution.py:229
  601.1 56.6 %collective-permute-start.153 = (bf16[1024,512]{1,0:T(8,128)(2,1)S(1)}, bf16[1024,512]{1,0:T(8,128)(2,1)S(1)}, u32[]{:S(2)}, u32[]{:S(2)}) collective-permute-start(bf16[1024,512]{1,0:T(8,128)(2,1)S(1)} %slice.822), channel_id=1, source_target_pairs={{0,4},{4,0},{1,5},{5,1},{2,6},{6,2},{3,7},{7,3},{8,12},{12,8},{9,1... | collective-permute-start | bytes 3145736 | tf_op jit(solution)/shard_map/ppermute | solution.py:229
  662.0 97.8 %collective-permute-start.76 = (bf16[64,2048]{1,0:T(8,128)(2,1)}, bf16[64,2048]{1,0:T(8,128)(2,1)}, u32[]{:S(2)}, u32[]{:S(2)}) collective-permute-start(bf16[64,2048]{1,0:T(8,128)(2,1)} %get-tuple-element.296), channel_id=1, source_target_pairs={{0,2},{2,0},{1,3},{3,1},{4,6},{6,4},{5,7},{7,5},{8,10},{10,8},{9,1... | collective-permute-start | bytes 786440 | tf_op jit(solution)/shard_map/ppermute | solution.py:229
  842.7 55.8 %collective-permute-start.138 = (bf16[1024,512]{1,0:T(8,128)(2,1)}, bf16[1024,512]{1,0:T(8,128)(2,1)}, u32[]{:S(2)}, u32[]{:S(2)}) collective-permute-start(bf16[1024,512]{1,0:T(8,128)(2,1)} %slice.792), channel_id=1, source_target_pairs={{0,4},{4,0},{1,5},{5,1},{2,6},{6,2},{3,7},{7,3},{8,12},{12,8},{9,1... | collective-permute-start | bytes 3145736 | tf_op jit(solution)/shard_map/ppermute | solution.py:229
  857.5 58.8 %collective-permute-start.142 = (bf16[512,512]{1,0:T(8,128)(2,1)}, bf16[512,512]{1,0:T(8,128)(2,1)}, u32[]{:S(2)}, u32[]{:S(2)}) collective-permute-start(bf16[512,512]{1,0:T(8,128)(2,1)} %slice.800), channel_id=1, source_target_pairs={{0,16},{16,0},{1,17},{17,1},{2,18},{18,2},{3,19},{19,3},{4,20},{20... | collective-permute-start | bytes 1572872 | tf_op jit(solution)/shard_map/ppermute | solution.py:229
  962.9 120.2 %collective-permute-start.132 = (bf16[1024,512]{1,0:T(8,128)(2,1)}, bf16[1024,512]{1,0:T(8,128)(2,1)}, u32[]{:S(2)}, u32[]{:S(2)}) collective-permute-start(bf16[1024,512]{1,0:T(8,128)(2,1)} %slice.780), channel_id=1, source_target_pairs={{0,4},{4,0},{1,5},{5,1},{2,6},{6,2},{3,7},{7,3},{8,12},{12,8},{9,1... | collective-permute-start | bytes 3145736 | tf_op jit(solution)/shard_map/ppermute | solution.py:229
  1028.0 59.6 %collective-permute-start.126 = (bf16[1024,512]{1,0:T(8,128)(2,1)}, bf16[1024,512]{1,0:T(8,128)(2,1)}, u32[]{:S(2)}, u32[]{:S(2)}) collective-permute-start(bf16[1024,512]{1,0:T(8,128)(2,1)} %slice.766), channel_id=1, source_target_pairs={{0,4},{4,0},{1,5},{5,1},{2,6},{6,2},{3,7},{7,3},{8,12},{12,8},{9,1... | collective-permute-start | bytes 3145736 | tf_op jit(solution)/shard_map/ppermute | solution.py:229
  1043.3 57.2 %collective-permute-start.123 = (bf16[1024,512]{1,0:T(8,128)(2,1)S(1)}, bf16[1024,512]{1,0:T(8,128)(2,1)S(1)}, u32[]{:S(2)}, u32[]{:S(2)}) collective-permute-start(bf16[1024,512]{1,0:T(8,128)(2,1)S(1)} %slice.760), channel_id=1, source_target_pairs={{0,4},{4,0},{1,5},{5,1},{2,6},{6,2},{3,7},{7,3},{8,12},{12,8},{9,1... | collective-permute-start | bytes 3145736 | tf_op jit(solution)/shard_map/ppermute | solution.py:229
  1090.1 77.6 %collective-permute-start.127 = (bf16[512,512]{1,0:T(8,128)(2,1)}, bf16[512,512]{1,0:T(8,128)(2,1)}, u32[]{:S(2)}, u32[]{:S(2)}) collective-permute-start(bf16[512,512]{1,0:T(8,128)(2,1)} %slice.768), channel_id=1, source_target_pairs={{0,16},{16,0},{1,17},{17,1},{2,18},{18,2},{3,19},{19,3},{4,20},{20... | collective-permute-start | bytes 1572872 | tf_op jit(solution)/shard_map/ppermute | solution.py:229
  1101.7 80.8 %collective-permute-start.124 = (bf16[512,512]{1,0:T(8,128)(2,1)}, bf16[512,512]{1,0:T(8,128)(2,1)}, u32[]{:S(2)}, u32[]{:S(2)}) collective-permute-start(bf16[512,512]{1,0:T(8,128)(2,1)} %slice.762), channel_id=1, source_target_pairs={{0,16},{16,0},{1,17},{17,1},{2,18},{18,2},{3,19},{19,3},{4,20},{20... | collective-permute-start | bytes 1572872 | tf_op jit(solution)/shard_map/ppermute | solution.py:229
  (331 other events, 6326.2 us)
where the time goes:
time: 1220 us; the launch traced here: 1210 us
  waiting for transfers between devices  562 us (46%)
  starting transfers between devices  194 us (16%)
  local copies, waits for them, and re-layouts  156 us (13%)
  other arithmetic  104 us (9%)
  blocking collectives  66.9 us (5%)
  matrix products  63.3 us (5%)
  Pallas kernels  57.1 us (5%)
    ppermute x143, waiting for transfers between devices, exchange(): return lax.ppermute(value, axis, SWAP)  542 us
    ppermute x143, starting transfers between devices, exchange(): return lax.ppermute(value, axis, SWAP)  170 us
    unnamed x438, local copies, waits for them, and re-layouts  53.7 us
    pallas_call x1, Pallas kernels, scan_backward(): pl.pallas_call(scan_backward_kernel, grid=(n,), in_specs=[act, act, act,...  46 us
    all_gather x1, blocking collectives, shards(): lax.all_gather(mixer_select, dp_axes, axis=0, tiled=True)  33.9 us
    all_gather x1, blocking collectives, shards(): step_weight = mine(lax.all_gather(mixer_step, dp_axes, axis=0, tiled=True))  33 us
  transfers between devices with their start and end apart: 159, of which 71 were waited for; matrix products, arithmetic and copies ran while one was open for 24% of the time, Pallas kernels for 5%

commit v1 on v0

v1 whole, which is shorter than its diff:
```python
import functools
import jax
import jax.numpy as jnp
from jax import lax
from jax.experimental import pallas as pl
from jax.experimental.pallas import tpu as pltpu
from jax.sharding import PartitionSpec as P

HEAD_DIM = 64
WINDOW = 2048
EPS = 1e-05
ROPE_BASE = 10000.0
MASKED = -1e30
BF = jnp.bfloat16
F32 = jnp.float32
SWAP = ((0, 1), (1, 0))
QUARTERS = 4
LANES = 128
ROWS = 8


def scan_forward_kernel(
    place_ref, x_ref, raw_ref, gate_ref, sel_ref, bias_ref, decay_ref, skip_ref, y_ref, gated_ref, hist_ref, state_ref
):
    seqs, steps, channels = x_ref.shape
    blocks = channels // LANES
    states_n = decay_ref.shape[0]
    pairs = [(s, j) for s in range(seqs) for j in range(blocks)]

    @pl.when(pl.program_id(1) == 0)
    def _():
        state_ref[...] = jnp.zeros_like(state_ref)

    def lanes(j):
        return slice(j * LANES, (j + 1) * LANES)

    rates = [-jnp.exp(decay_ref[:, lanes(j)]) for j in range(blocks)]

    def chunk(k, states):
        states = list(states)
        rows = pl.ds(pl.multiple_of(k * ROWS, ROWS), ROWS)
        x_t, d_t, dx_t = {}, {}, {}
        for s, j in pairs:
            x_t[s, j] = x_ref[s, rows, lanes(j)]
            d_t[s, j] = jax.nn.softplus(raw_ref[s, rows, lanes(j)] + bias_ref[:, lanes(j)])
            dx_t[s, j] = d_t[s, j] * x_t[s, j]
        outs = {p: [] for p in pairs}
        for i in range(ROWS):
            for s in range(seqs):
                sel_b = jnp.broadcast_to(sel_ref[s, k, :states_n, i : i + 1], (states_n, LANES))
                sel_c = jnp.broadcast_to(sel_ref[s, k, states_n:, i : i + 1], (states_n, LANES))
                for j in range(blocks):
                    at = s * blocks + j
                    before = states[at]
                    hist_ref[s, k * ROWS + i, :, lanes(j)] = before
                    factor = jnp.exp(d_t[s, j][i : i + 1] * rates[j])
                    after = factor * before + dx_t[s, j][i : i + 1] * sel_b
                    states[at] = after
                    outs[s, j].append(jnp.sum(after * sel_c, axis=0, keepdims=True))
        for s, j in pairs:
            y = jnp.concatenate(outs[s, j], axis=0) + skip_ref[:, lanes(j)] * x_t[s, j]
            gate = gate_ref[0, s, 0, rows, lanes(j)]
            y_ref[s, rows, lanes(j)] = y
            gated_ref[0, s, 0, rows, lanes(j)] = y * gate * jax.nn.sigmoid(gate)
        return tuple(states)

    first = tuple(state_ref[s * blocks + j] for s, j in pairs)
    last = lax.fori_loop(0, steps // ROWS, chunk, first)
    for at, value in enumerate(last):
        state_ref[at] = value


def group_sums(states_n):
    shape = (ROWS, ROWS * states_n)
    step = lax.broadcasted_iota(jnp.int32, shape, 1) // states_n
    return (step == lax.broadcasted_iota(jnp.int32, shape, 0)).astype(jnp.bfloat16)


def scan_backward_kernel(
    place_ref, x_ref, raw_ref, gate_ref, y_ref, grad_ref, hist_ref, sel_ref, bias_ref, decay_ref, skip_ref,
    dgate_ref, dx_ref, draw_ref, dsel_ref, ddecay_ref, dskip_ref, dbias_ref,
    adj_ref, step_ref, drive_ref, out_ref, first_ref, second_ref, db_ref, dc_ref,
):
    _, steps, channels = x_ref.shape
    blocks = channels // LANES
    states_n = decay_ref.shape[0]

    @pl.when(pl.program_id(1) == 0)
    def _():
        adj_ref[...] = jnp.zeros_like(adj_ref)

    @pl.when((pl.program_id(0) == 0) & (pl.program_id(1) == 0))
    def _():
        ddecay_ref[...] = jnp.zeros_like(ddecay_ref)
        dskip_ref[...] = jnp.zeros_like(dskip_ref)
        dbias_ref[...] = jnp.zeros_like(dbias_ref)

    def lanes(j):
        return slice(j * LANES, (j + 1) * LANES)

    rates = [-jnp.exp(decay_ref[:, lanes(j)]) for j in range(blocks)]
    sums = group_sums(states_n)
    ones = jnp.ones((ROWS, LANES), jnp.bfloat16)
    over_lanes = lambda v: lax.dot_general(ones, v, (((1,), (1,)), ((), ())), preferred_element_type=jnp.float32)

    def chunk(step, carry):
        adjoint, decay_sum = list(carry[0]), list(carry[1])
        k = steps // ROWS - 1 - step
        rows = pl.ds(pl.multiple_of(k * ROWS, ROWS), ROWS)
        x = x_ref[0, rows, :]
        z = raw_ref[0, rows, :] + bias_ref[...]
        delta = jax.nn.softplus(z)
        gate = gate_ref[0, 0, 0, rows, :]
        sig = jax.nn.sigmoid(gate)
        grad = grad_ref[0, 0, 0, rows, :]
        dy = grad * gate * sig
        dgate_ref[0, 0, 0, rows, :] = grad * y_ref[0, rows, :] * sig * (1.0 + gate * (1.0 - sig))
        step_ref[...] = delta
        drive_ref[...] = delta * x
        out_ref[...] = dy
        for i in reversed(range(ROWS)):
            place = slice(i * states_n, (i + 1) * states_n)
            sel_b = jnp.broadcast_to(sel_ref[0, k, :states_n, i : i + 1], (states_n, LANES))
            sel_c = jnp.broadcast_to(sel_ref[0, k, states_n:, i : i + 1], (states_n, LANES))
            db = jnp.zeros((states_n, LANES), jnp.float32)
            dc = jnp.zeros((states_n, LANES), jnp.float32)
            for j in range(blocks):
                before = hist_ref[0, k * ROWS + i, :, lanes(j)]
                width = step_ref[i : i + 1, lanes(j)]
                drive = drive_ref[i : i + 1, lanes(j)]
                out = out_ref[i : i + 1, lanes(j)]
                factor = jnp.exp(width * rates[j])
                after = factor * before + drive * sel_b
                lam = adjoint[j] + out * sel_c
                dc = dc + out * after
                db = db + drive * lam
                first_ref[place, lanes(j)] = (lam * sel_b).astype(jnp.bfloat16)
                back = lam * factor
                adjoint[j] = back
                through = back * before
                second_ref[place, lanes(j)] = (rates[j] * through).astype(jnp.bfloat16)
                decay_sum[j] = decay_sum[j] + width * through
            db_ref[place, :] = db.astype(jnp.bfloat16)
            dc_ref[place, :] = dc.astype(jnp.bfloat16)
        dsel_ref[0, k, 0:ROWS, :] = over_lanes(db_ref[...])
        dsel_ref[0, k, ROWS : 2 * ROWS, :] = over_lanes(dc_ref[...])
        one = jnp.dot(sums, first_ref[...], preferred_element_type=jnp.float32)
        two = jnp.dot(sums, second_ref[...], preferred_element_type=jnp.float32)
        dx_ref[0, rows, :] = dy * skip_ref[...] + delta * one
        draw = (two + x * one) * jax.nn.sigmoid(z)
        draw_ref[0, rows, :] = draw
        dskip_ref[...] += dy * x
        dbias_ref[...] += draw
        return tuple(adjoint), tuple(decay_sum)

    carry = (
        tuple(adj_ref[j] for j in range(blocks)),
        tuple(jnp.zeros((states_n, LANES), jnp.float32) for _ in range(blocks)),
    )
    adjoint, decay_sum = lax.fori_loop(0, steps // ROWS, chunk, carry, unroll=2)
    for j in range(blocks):
        adj_ref[j] = adjoint[j]
        ddecay_ref[:, lanes(j)] += rates[j] * decay_sum[j]


def quarter_block(place, quarter):
    return place[1] ^ (quarter & 1), place[0] ^ (quarter >> 1)


def scan_call(kernel, name, ins, outs, sel, vectors, place, reverse, extra_outs=(), scratch=()):
    seqs, length, channels = ins[0][1].shape
    states_n = vectors[1].shape[0]
    steps = length // QUARTERS
    turn = lambda i: QUARTERS - 1 - i if reverse else i

    def spec(kind, width):
        if kind == "time":
            return pl.BlockSpec((1, steps, width), lambda s, i, place: (s, turn(i), 0))
        if kind == "hist":
            return pl.BlockSpec((1, steps, states_n, width), lambda s, i, place: (s, turn(i), 0, 0))
        if kind == "dsel":
            return pl.BlockSpec((1, steps // ROWS, 2 * ROWS, ROWS * states_n), lambda s, i, place: (s, turn(i), 0, 0))
        if kind == "sel":
            return pl.BlockSpec((1, steps // ROWS, 2 * states_n, ROWS), lambda s, i, place: (s, turn(i), 0, 0))
        return pl.BlockSpec(
            (1, 1, 1, steps, width),
            lambda s, i, place: (quarter_block(place, turn(i))[0], s, quarter_block(place, turn(i))[1], 0, 0),
        )

    whole = lambda shape: pl.BlockSpec(shape, lambda s, i, place: (0,) * len(shape))
    shape_of = {
        "time": (seqs, length, channels),
        "hist": (seqs, length, states_n, channels),
        "dsel": sel.shape[:2] + (2 * ROWS, ROWS * states_n),
        "mine": (2, seqs, 2, steps, channels),
    }
    elems = seqs * length * channels * states_n
    full = lambda shape: jax.ShapeDtypeStruct(shape, jnp.float32)
    return pl.pallas_call(
        kernel,
        grid_spec=pltpu.PrefetchScalarGridSpec(
            num_scalar_prefetch=1,
            grid=(seqs, QUARTERS),
            in_specs=[spec(kind, channels) for kind, _ in ins] + [spec("sel", 0)] + [whole(v.shape) for v in vectors],
            out_specs=[spec(kind, channels) for kind in outs] + [whole(shape) for shape in extra_outs],
            scratch_shapes=[pltpu.VMEM((channels // LANES, states_n, LANES), jnp.float32)] + list(scratch),
        ),
        out_shape=[full(shape_of[kind]) for kind in outs] + [full(shape) for shape in extra_outs],
        cost_estimate=pl.CostEstimate(
            flops=(60 if reverse else 20) * elems, bytes_accessed=4 * elems, transcendentals=elems
        ),
        compiler_params=pltpu.CompilerParams(vmem_limit_bytes=48 * 1024 * 1024),
        name=name,
    )(place, *[v for _, v in ins], sel, *vectors)


def scan_forward(x, raw, gate, sel, bias, decay, skip, place):
    ins = (("time", x), ("time", raw), ("mine", gate))
    vectors = (bias.reshape(1, -1), decay, skip.reshape(1, -1))
    return scan_call(scan_forward_kernel, "scan_forward", ins, ("time", "mine", "hist"), sel, vectors, place, False)


def scan_backward(x, raw, gate, y, grad, hist, sel, bias, decay, skip, place):
    ins = (("time", x), ("time", raw), ("mine", gate), ("time", y), ("mine", grad), ("hist", hist))
    vectors = (bias.reshape(1, -1), decay, skip.reshape(1, -1))
    extra = (decay.shape, (ROWS, x.shape[2]), (ROWS, x.shape[2]))
    group, channels = ROWS * decay.shape[0], x.shape[2]
    scratch = (
        [pltpu.VMEM((ROWS, channels), jnp.float32)] * 3
        + [pltpu.VMEM((group, channels), jnp.bfloat16)] * 2
        + [pltpu.VMEM((group, LANES), jnp.bfloat16)] * 2
    )
    outs = ("mine", "time", "time", "dsel")
    return scan_call(scan_backward_kernel, "scan_backward", ins, outs, sel, vectors, place, True, extra, scratch)


def turn_heads(value, cosine, sine):
    size = value.shape[1]
    half = HEAD_DIM // 2
    lane = lax.broadcasted_iota(jnp.int32, value.shape, 1)
    partner = jnp.where(lane % HEAD_DIM < half, pltpu.roll(value, size - half, 1), pltpu.roll(value, half, 1))
    return value * cosine + partner * sine


def head_pair(ref, part, pair, pairs):
    at = (part * pairs + pair) * LANES
    return ref[:, 0, :, :, at : at + LANES].reshape(-1, LANES)


def pair_weights(queries, keys, head_lanes, mask):
    zero = jnp.zeros_like(queries)
    scores = lax.dot_general(
        jnp.where(head_lanes, queries, zero), keys, (((1,), (1,)), ((), ())), preferred_element_type=jnp.float32
    )
    scores = jnp.where(mask, scores * HEAD_DIM**-0.5, MASKED)
    raised = jnp.exp(scores - jnp.max(scores, axis=1, keepdims=True))
    return raised / jnp.sum(raised, axis=1, keepdims=True)


def attention_forward_kernel(triple_ref, cos_ref, sin_ref, row_ref, col_ref, turned_ref, context_ref):
    pairs = context_ref.shape[-1] // LANES
    shape = context_ref.shape[:-1] + (LANES,)
    mask = (col_ref[...] <= row_ref[...]) & (row_ref[...] - col_ref[...] < WINDOW)
    cosine, sine = cos_ref[...], sin_ref[...]
    low_lanes = lax.broadcasted_iota(jnp.int32, (1, LANES), 1) < HEAD_DIM
    for pair in range(pairs):
        queries = turn_heads(head_pair(triple_ref, 0, pair, pairs), cosine, sine).astype(jnp.bfloat16)
        keys = turn_heads(head_pair(triple_ref, 1, pair, pairs), cosine, sine).astype(jnp.bfloat16)
        values = head_pair(triple_ref, 2, pair, pairs).astype(jnp.bfloat16)
        outs = []
        for head in range(LANES // HEAD_DIM):
            lanes = low_lanes if head == 0 else ~low_lanes
            attend = pair_weights(queries, keys, lanes, mask).astype(jnp.bfloat16)
            outs.append(jnp.dot(attend, values, preferred_element_type=jnp.float32))
        context = jnp.where(low_lanes, outs[0], outs[1]).astype(jnp.bfloat16)
        context_ref[..., pair * LANES : (pair + 1) * LANES] = context.reshape(shape)
        for part, value in enumerate((queries, keys, values)):
            at = (part * pairs + pair) * LANES
            turned_ref[..., at : at + LANES] = value.reshape(shape)


def attention_backward_kernel(turned_ref, grad_ref, cos_ref, sin_ref, row_ref, col_ref, out_ref):
    pairs = grad_ref.shape[-1] // LANES
    shape = grad_ref.shape[:-1] + (LANES,)
    mask = (col_ref[...] <= row_ref[...]) & (row_ref[...] - col_ref[...] < WINDOW)
    cosine, sine = cos_ref[...], -sin_ref[...]
    low_lanes = lax.broadcasted_iota(jnp.int32, (1, LANES), 1) < HEAD_DIM
    dot = lambda a, b, dims: lax.dot_general(a, b, (dims, ((), ())), preferred_element_type=jnp.float32)
    for pair in range(pairs):
        queries, keys, values = (head_pair(turned_ref, part, pair, pairs) for part in range(3))
        grads = head_pair(grad_ref, 0, pair, pairs)
        parts = [[], [], []]
        for head in range(LANES // HEAD_DIM):
            lanes = low_lanes if head == 0 else ~low_lanes
            full = pair_weights(queries, keys, lanes, mask)
            attend = full.astype(jnp.bfloat16)
            own = jnp.where(lanes, grads, jnp.zeros_like(grads))
            weight_grad = dot(own, values, ((1,), (1,)))
            delta = jnp.sum(full * weight_grad, axis=1, keepdims=True)
            score_grad = (full * (weight_grad - delta)).astype(jnp.bfloat16)
            parts[0].append(dot(score_grad, keys, ((1,), (0,))) * HEAD_DIM**-0.5)
            parts[1].append(dot(score_grad, queries, ((0,), (0,))) * HEAD_DIM**-0.5)
            parts[2].append(dot(attend, grads, ((0,), (0,))))
        for part, (low, high) in enumerate(parts):
            value = jnp.where(low_lanes, low, high)
            if part < 2:
                value = turn_heads(value, cosine, sine)
            at = (part * pairs + pair) * LANES
            out_ref[..., at : at + LANES] = value.astype(jnp.bfloat16).reshape(shape)


def rotary_tables(positions):
    half = HEAD_DIM // 2
    frequency = ROPE_BASE ** (-jnp.arange(half, dtype=F32) * 2.0 / HEAD_DIM)
    angles = positions.astype(F32)[:, None] * frequency[None, :]
    cosine, sine = jnp.cos(angles), jnp.sin(angles)
    twice = lambda low, high: jnp.concatenate([low, high] * (LANES // HEAD_DIM), axis=1)
    return twice(cosine, cosine), twice(-sine, sine), positions[:, None], positions[None, :]


def attention_call(kernel, name, ins, widths, tables):
    lead = ins[0].shape[:-1]
    split = lambda width: pl.BlockSpec((lead[0], 1) + lead[2:] + (width,), lambda s: (0, s, 0, 0, 0))
    whole = lambda a: pl.BlockSpec(a.shape, lambda s: (0, 0))
    length = lead[0] * lead[2] * lead[3]
    heads = widths[-1] // HEAD_DIM
    flops = 2 * lead[1] * 2 * length * length * LANES * 5 * max(heads, 1)
    return pl.pallas_call(
        kernel,
        grid=(lead[1],),
        in_specs=[split(a.shape[-1]) for a in ins] + [whole(t) for t in tables],
        out_specs=[split(w) for w in widths],
        out_shape=[jax.ShapeDtypeStruct(lead + (w,), jnp.bfloat16) for w in widths],
        cost_estimate=pl.CostEstimate(flops=flops, bytes_accessed=4 * 1024 * 1024, transcendentals=length * length * 8),
        compiler_params=pltpu.CompilerParams(vmem_limit_bytes=32 * 1024 * 1024),
        name=name,
    )(*ins, *tables)


def bit(axis):
    return lax.axis_index(axis)


def exchange(value, axis):
    return lax.ppermute(value, axis, SWAP)


def exchange_diagonal(value):
    return lax.ppermute(value, ("b", "x"), ((0, 3), (1, 2), (2, 1), (3, 0)))


def ordered(axis, mine, other):
    first = bit(axis) == 0
    return lax.select(first, mine, other), lax.select(first, other, mine)


def half_of(value, axis, other=False):
    width = value.shape[-1] // 2
    at = bit(axis) if not other else 1 - bit(axis)
    return lax.dynamic_slice_in_dim(value, at * width, width, axis=value.ndim - 1)


def tied(value, *tokens):
    return lax.optimization_barrier((value,) + tokens)[0]


class Pump:
    def __init__(self, layout):
        self.layout, self.waiting, self.flying = layout, [], []

    def add(self, job):
        self.waiting.append(job)

    def land(self, token):
        token, flying = lax.optimization_barrier((token, [results for _, results in self.flying]))
        self.flying = [(job, results) for (job, _), results in zip(self.flying, flying)]
        return token

    def turn(self, token, count=1, hold=0):
        split = len(self.flying) - hold
        going, held = self.flying[:split], self.flying[split:]
        if going:
            flat = [r for _, results in going for r in results]
            tied_all = lax.optimization_barrier((token, *flat))
            token, flat = tied_all[0], list(tied_all[1:])
        asks = []
        for job, results in going:
            got, flat = flat[: len(results)], flat[len(results) :]
            try:
                asks.append((job, job.send(got)))
            except StopIteration:
                pass
        for job in self.waiting[:count]:
            asks.append((job, [(tied(v, token), axis) for v, axis in next(job)]))
        del self.waiting[:count]
        self.flying = held + [(job, [exchange(v, axis) for v, axis in ask]) for job, ask in asks]
        return token

    def begin(self, token, count=1):
        for job in self.waiting[:count]:
            self.flying.append((job, [exchange(tied(v, token), axis) for v, axis in next(job)]))
        del self.waiting[:count]

    def until(self, token, store, *names):
        while not all(name in store for name in names):
            token = self.turn(token)
        return token

    def flush(self):
        jobs = [(job, [exchange(v, axis) for v, axis in next(job)]) for job in self.waiting]
        for job, results in self.flying + jobs:
            try:
                while True:
                    results = [exchange(v, axis) for v, axis in job.send(list(results))]
            except StopIteration:
                pass
        self.waiting, self.flying = [], []


class Layout:
    def __init__(self, high):
        self.high = high
        self.sums = high + ("y",)

    def split_bits(self, value, at):
        k = len(self.high) + 2
        return value.reshape(value.shape[:at] + (2,) * k + (value.shape[at] >> k,) + value.shape[at + 1 :])

    def turned(self, value, at):
        for place, axis in enumerate(self.high + ("b", "y")):
            if axis != "b":
                value = lax.select(bit(axis) == 0, value, lax.rev(value, (at + place,)))
        return value

    def columns_in(self, value, at=-1):
        shape, at = value.shape, at % value.ndim
        value = self.turned(self.split_bits(value, at), at)
        return jnp.moveaxis(value, at + len(self.high) + 1, at).reshape(shape)

    def columns_out(self, value, at=-1):
        shape, at = value.shape, at % value.ndim
        value = jnp.moveaxis(self.split_bits(value, at), at, at + len(self.high) + 1)
        return self.turned(value, at).reshape(shape)


def fetch_job(layout, mine, other, store, name):
    own = jnp.concatenate(ordered("b", mine, other), axis=0)
    axes = layout.high[::-1]
    if len(axes) == 1:
        high, beside = yield [(own, axes[0]), (own, "y")]
        (far,) = yield [(high, "y")]
        pieces = [own, high, beside, far]
    else:
        pieces = [own]
        for axis in axes + ("y",):
            got = yield [(piece, axis) for piece in pieces]
            pieces = pieces + list(got)
    store[name] = jnp.concatenate(pieces, axis=0)


def settle_job(layout, left, right, store, name):
    width = left.shape[1]
    got = []
    product = lambda lo, hi: sum((g[lo:hi].astype(F32) for g in got), mm_tn(left[:, lo:hi], right))
    for axis in ("y",) + layout.high:
        width = width // 2
        got += yield [(product(width, 2 * width).astype(BF), axis)]
    total = product(0, width).astype(BF)
    keep, send = ordered("b", total[: width // 2], total[width // 2 :])
    (other,) = yield [(send, "b")]
    store[name] = ordered("b", keep, other)


def small_job(layout, value, store, name):
    for axis in layout.sums:
        (got,) = yield [(value.astype(BF), axis)]
        value = value + got.astype(F32)
    (got,) = yield [(value.astype(BF), "b")]
    store[name] = jnp.concatenate(ordered("b", value, got.astype(F32)), axis=1)


def gather_rows(rows):
    with jax.named_scope("rows_gather"):
        beside = exchange(rows, "x")
        across = exchange(rows, "b")
        corner = exchange_diagonal(rows)
        mine = jnp.concatenate([rows, beside, across, corner], axis=-2)
        return jnp.concatenate([mine, exchange(mine, "c")], axis=-2)


def scatter_rows(products):
    with jax.named_scope("rows_scatter"):
        half = products[0][0].shape[0] // 2
        send = sum(mm_nt(v[half:], w) for v, w in products).astype(BF)
        got = exchange(send, "c")
        keep = sum(mm_nt(v[:half], w) for v, w in products) + got.astype(F32)
        rows = half // 4
        low = keep[rows:].astype(BF)
        beside = exchange(low[:rows], "x")
        across = exchange(low[rows : 2 * rows], "b")
        corner = exchange_diagonal(low[2 * rows :])
        return keep[:rows] + beside.astype(F32) + across.astype(F32) + corner.astype(F32)


def in_time(value):
    left, right = ordered("x", value[:, :, 0], value[:, :, 1])
    halves = [jnp.stack(ordered("c", half[0], half[1]), axis=1) for half in (left, right)]
    return jnp.stack(halves, axis=1).reshape(value.shape[1], -1, value.shape[-1])


def from_time(value, rows):
    value = value.reshape(value.shape[0], 2, 2, rows, value.shape[-1])
    parts = [jnp.stack(ordered("x", v[:, 0], v[:, 1]), axis=1) for v in ordered("c", value[:, :, 0], value[:, :, 1])]
    return jnp.stack(parts)


def gather_sequence(rows):
    even, odd = ordered("c", rows, exchange(rows, "c"))
    pair = jnp.stack([even, odd])
    left, right = ordered("x", pair, exchange(pair, "x"))
    return jnp.stack([left, right]).reshape(QUARTERS * rows.shape[0], -1)


def channel_total(partial, low=False):
    narrow = (lambda v: v.astype(BF)) if low else (lambda v: v)
    total = partial + exchange(narrow(partial), "c").astype(F32)
    return chip_total(total, narrow)


def chip_total(total, narrow=lambda v: v.astype(BF)):
    total = total + exchange(narrow(total), "x").astype(F32)
    other = exchange(narrow(total), "b").astype(F32)
    rows = total.shape[0] // 2
    return total + jnp.concatenate([other[rows:], other[:rows]], axis=0)


def rms(stream, gain_row):
    scale = lax.rsqrt(jnp.mean(stream * stream, axis=-1, keepdims=True) + EPS)
    return (stream * scale * gain_row[None, :]).astype(BF)


def rms_back(stream, gain_row, grad):
    scale = lax.rsqrt(jnp.mean(stream * stream, axis=-1, keepdims=True) + EPS)
    gain_grad = jnp.sum(grad * stream * scale, axis=0)
    scaled = grad * gain_row[None, :]
    inner = jnp.mean(scaled * stream, axis=-1, keepdims=True)
    return scale * scaled - stream * (scale * scale * scale * inner), gain_grad


def mm(left, right):
    return jnp.dot(left, right, preferred_element_type=F32)


def mm_nt(left, right):
    return lax.dot_general(left, right, (((1,), (1,)), ((), ())), preferred_element_type=F32)


def mm_tn(left, right):
    return lax.dot_general(left, right, (((0,), (0,)), ((), ())), preferred_element_type=F32)


def conv_total(inner, taps, bias):
    count, length = taps.shape[0], inner.shape[1]
    padded = jnp.pad(inner, ((0, 0), (count - 1, 0), (0, 0)))
    total = bias[None, None, :]
    for k in range(count):
        total = total + taps[k][None, None, :] * padded[:, k : k + length]
    return total


def conv_back(grad, inner, taps):
    count, length = taps.shape[0], inner.shape[1]
    before = jnp.pad(inner, ((0, 0), (count - 1, 0), (0, 0)))
    after = jnp.pad(grad, ((0, 0), (0, count - 1), (0, 0)))
    inner_grad = 0.0
    taps_grad = []
    for k in range(count):
        shift = count - 1 - k
        inner_grad = inner_grad + taps[k][None, None, :] * after[:, shift : shift + length]
        taps_grad.append(jnp.sum(grad * before[:, k : k + length], axis=(0, 1)))
    return inner_grad, jnp.stack(taps_grad), jnp.sum(grad, axis=(0, 1))


def mixer_backward(stored, low_grad, weights, channel, place, pump, store):
    inner_weight, gate_weight, out_weight, select_weight, step_weight = weights
    taps, conv_bias, step_bias, decay_log, skip_gain = channel
    normed, inner, gate, conv_out, step_low, raw, sel, mixed, gated, hist = stored
    tokens = normed.shape[0]
    rows = tokens // 8
    flat = lambda v: v.reshape(tokens, -1)
    gated_grad = mm(low_grad, out_weight)
    gated_grad = gated_grad.reshape(gate.shape)
    from_scan = scan_backward(
        conv_out.astype(F32), raw, gate, mixed, gated_grad, hist, sel, step_bias, decay_log, skip_gain, place
    )
    gate_grad, conv_scan, raw_grad, sel_grad, decay_grad, skip_grad, bias_grad = pump.land(tuple(from_scan))

    raw_low = flat(raw_grad).astype(BF)
    step_low_grad = mm_nt(raw_low, step_weight)
    states = [sel_grad[:, :, at].reshape(tokens, -1) for at in (0, ROWS)]
    select_grads = jnp.concatenate([step_low_grad, *states], axis=1)
    gate_low = flat(gate_grad.astype(BF))
    pump.add(settle_job(pump.layout, normed, gate_low, store, "gate"))
    with jax.named_scope("select_return"):
        select_grads = select_grads + exchange(select_grads.astype(BF), "c").astype(F32)
        select_grads = pump.turn(select_grads, 1)
        select_low = chip_total(select_grads).astype(BF)
    select_low = pump.turn(select_low, 0)
    conv_grad = conv_scan + mm(select_low, select_weight).reshape(conv_scan.shape)
    before = conv_total(inner, taps, conv_bias)
    sig = jax.nn.sigmoid(before)
    inner_grad, taps_grad, conv_bias_grad = conv_back(conv_grad * sig * (1.0 + before * (1.0 - sig)), inner, taps)
    inner_low = flat(from_time(inner_grad.astype(BF), rows))
    cut = inner_low.shape[1] // 2
    inner_parts = (inner_low[:, :cut], inner_low[:, cut:])
    for name, part in zip(("inner0", "inner1"), inner_parts):
        pump.add(settle_job(pump.layout, normed, part, store, name))
    small = jnp.concatenate(
        [
            mm_tn(select_low, flat(conv_out)),
            mm_tn(step_low, raw_low),
            taps_grad,
            conv_bias_grad[None],
            jnp.sum(bias_grad, axis=0, keepdims=True),
            decay_grad,
            jnp.sum(skip_grad, axis=0, keepdims=True),
        ],
        axis=0,
    )
    pump.add(small_job(pump.layout, small, store, "small"))
    pump.begin(inner_low, 3)
    return (*zip(inner_parts, inner_weight), (gate_low, gate_weight))


def ffn_backward(stored, low_grad, weights):
    gate_weight, up_weight, down_weight = weights
    normed, gate, up, hidden = stored
    hidden_grad = mm(low_grad, down_weight)
    sig = jax.nn.sigmoid(gate)
    gate_low = (hidden_grad * up * sig * (1.0 + gate * (1.0 - sig))).astype(BF)
    up_low = (hidden_grad * gate * sig).astype(BF)
    return [(gate_low, gate_weight), (up_low, up_weight)]


def shards(
    layout,
    layer_input,
    upstream,
    norm_gains,
    mixer_input,
    conv_taps,
    conv_bias,
    mixer_select,
    mixer_step,
    step_bias,
    decay_log,
    skip_gain,
    mixer_output,
    first_gate_up,
    first_down,
    attention_input,
    attention_output,
    second_gate_up,
    second_down,
):
    mine = lambda v: half_of(v, "b")
    theirs = lambda v: half_of(v, "b", True)
    place = jnp.stack([bit("x"), bit("c")]).astype(jnp.int32)
    quarter = place[0] * 2 + place[1]
    rows = layer_input.shape[0] // QUARTERS
    tokens = 8 * rows
    own_rows = lambda v: layout.columns_in(lax.dynamic_slice_in_dim(v, quarter * rows, rows, axis=0))
    blocks = lambda v: v.reshape(2, 2, 2, rows, v.shape[-1])

    pump, weights, grads = Pump(layout), {}, {}

    def swapped(arrays, *tokens):
        with jax.named_scope("pack"):
            if tokens:
                arrays = lax.optimization_barrier((tuple(arrays),) + tokens)[0]
            flat = lambda v: v.reshape(v.shape[0], -1)
            kept = jnp.concatenate([flat(mine(a)) for a in arrays], axis=1)
            return kept, exchange(jnp.concatenate([flat(theirs(a)) for a in arrays], axis=1), "b")

    def request(names, arrays, *tokens):
        kept, got = swapped(arrays, *tokens)
        width = kept.shape[1] // len(names)
        for at, name in enumerate(names):
            cut = slice(at * width, (at + 1) * width)
            pump.add(fetch_job(layout, kept[:, cut], got[:, cut], weights, name))
        return got

    here, _, wide = attention_input.shape
    width = wide // 2
    stream0 = own_rows(layer_input).astype(F32)
    gains = layout.columns_in(norm_gains)
    upstream_rows = own_rows(upstream)
    with jax.named_scope("inner_fetch"):
        first = request(["inner0", "inner1"], [mixer_input[:, 0]])
        pump.flush()
    normed0 = gather_rows(tied(rms(stream0, gains[0]), first))
    request(["small"], [jnp.concatenate([mixer_step, mixer_select], axis=0)], normed0)
    pump.flush()
    second = request(["gate", "out"], [mixer_input[:, 1], mixer_output], first)
    third = request(
        ["gate1", "up1", "down1"], [first_gate_up, first_down], normed0, second,
    )
    normed0 = pump.turn(normed0, 1)
    channel = tuple(mine(v) for v in (conv_taps, conv_bias, step_bias, decay_log, skip_gain))
    inner = jnp.concatenate([mm(normed0, weights["inner0"]), mm(normed0, weights["inner1"])], axis=1)
    inner = pump.turn(inner, 1)
    low4 = gather_rows(tied(upstream_rows, inner))
    inner = in_time(blocks(inner))
    conv_out = jax.nn.silu(conv_total(inner, channel[0], channel[1])).astype(BF)
    select_rows, step_rows = mixer_select.shape[0], mixer_step.shape[0]
    both = layout.columns_out(weights["small"], 0).reshape(-1, select_rows + step_rows, conv_out.shape[-1])
    select_weight = both[:, step_rows:].reshape(-1, conv_out.shape[-1])
    step_weight = both[:, :step_rows].reshape(-1, conv_out.shape[-1])
    partial = mm_nt(conv_out.reshape(tokens, -1), select_weight)
    with jax.named_scope("select_total"):
        selected = channel_total(partial, True)
    selected = pump.turn(selected)
    request(["query_key", "value_out"], [attention_input, attention_output], inner, third)
    rank, states_n = step_weight.shape[0], decay_log.shape[0]
    step_low = selected[:, :rank].astype(BF)
    raw = mm(step_low, step_weight).reshape(conv_out.shape)
    sel = selected[:, rank:].reshape(2, tokens // 2 // ROWS, ROWS, -1).transpose(0, 1, 3, 2)
    raw = pump.until(raw, weights, "gate")
    gate = blocks(mm(normed0, weights["gate"]))
    mixed, gated, hist = scan_forward(conv_out.astype(F32), raw, gate, sel, *channel[2:], place)
    gated = gated.reshape(tokens, -1).astype(BF)
    gated = pump.until(gated, weights, "out")
    mixer_stored = (normed0, inner, gate, conv_out, step_low, raw, sel, mixed, gated, hist)
    mixer_weights = ((weights["inner0"], weights["inner1"]), weights["gate"], weights["out"], select_weight, step_weight)
    stream1 = tied(pump.turn(stream0 + scatter_rows([(gated, weights["out"])])), low4)
    request(
        ["gate2", "up2", "down2"], [second_gate_up, second_down], gated
    )

    def ffn(normed, tag):
        normed = pump.until(normed, weights, "gate" + tag, "up" + tag)
        gate, up = mm(normed, weights["gate" + tag]), mm(normed, weights["up" + tag])
        hidden = (jax.nn.silu(gate) * up).astype(BF)
        return hidden, (normed, gate, up, hidden)

    hidden1, first_stored = ffn(pump.turn(gather_rows(rms(stream1, gains[1]))), "1")
    hidden1 = pump.until(hidden1, weights, "down1")
    first_weights = tuple(weights[n] for n in ("gate1", "up1", "down1"))
    stream2 = pump.turn(stream1 + scatter_rows([(hidden1, weights["down1"])]))

    normed2 = pump.turn(gather_rows(rms(stream2, gains[2])))
    normed2 = pump.until(normed2, weights, "query_key", "value_out")
    value_weight, out_weight = weights["value_out"][:, :width], weights["value_out"][:, width:]
    triple = jnp.concatenate([mm(normed2, weights["query_key"]), mm(normed2, value_weight)], axis=1)
    order = (jnp.arange(2)[None, :] ^ place[0]) * 2 + (jnp.arange(2)[:, None] ^ place[1])
    tables = rotary_tables((order[:, :, None] * rows + jnp.arange(rows)).reshape(-1))
    turned, context = attention_call(
        attention_forward_kernel, "attention_forward", [blocks(triple)], (3 * width, width), tables
    )
    context = context.reshape(tokens, -1)
    stream3 = pump.turn(stream2 + scatter_rows([(context, out_weight)]))

    hidden3, second_stored = ffn(gather_rows(rms(stream3, gains[3])), "2")
    hidden3 = pump.until(hidden3, weights, "down2")
    second_weights = tuple(weights[n] for n in ("gate2", "up2", "down2"))

    pump.add(settle_job(layout, low4, hidden3, grads, "down2"))
    pump.begin(hidden3, 1)
    products = ffn_backward(second_stored, low4, second_weights)
    normed3 = second_stored[0]
    for name, (right, _) in zip(("gate2", "up2"), products):
        pump.add(settle_job(layout, normed3, right, grads, name))
    back, gain3 = rms_back(stream3, gains[3], pump.turn(scatter_rows(products)))
    grad3 = upstream_rows.astype(F32) + back
    stream4 = stream3 + scatter_rows([(hidden3, weights["down2"])])

    low3 = gather_rows(grad3.astype(BF))
    pump.add(settle_job(layout, low3, context, grads, "attention_out"))
    low3 = pump.turn(low3, 2)
    context_grad = mm(low3, out_weight).astype(BF)
    (triple_low,) = attention_call(
        attention_backward_kernel, "attention_backward", [turned, blocks(context_grad)], (3 * width,), tables
    )
    triple_low = triple_low.reshape(tokens, -1)
    pump.add(settle_job(layout, normed2, triple_low, grads, "attention_in"))
    back, gain2 = rms_back(
        stream2,
        gains[2],
        pump.turn(
            scatter_rows([(triple_low[:, : 2 * width], weights["query_key"]), (triple_low[:, 2 * width :], value_weight)])
        ),
    )
    grad2 = grad3 + back
    low2 = pump.turn(gather_rows(grad2.astype(BF)), 0)
    products = ffn_backward(first_stored, low2, first_weights)
    pump.add(settle_job(layout, low2, first_stored[3], grads, "down1"))
    pump.begin(low2, 1)
    for name, (right, _) in zip(("gate1", "up1"), products):
        pump.add(settle_job(layout, first_stored[0], right, grads, name))
    back, gain1 = rms_back(stream1, gains[1], pump.turn(scatter_rows(products), 2))
    grad1 = grad2 + back

    low1 = gather_rows(grad1.astype(BF))
    pump.add(settle_job(layout, low1, mixer_stored[8], grads, "out"))
    low1 = pump.turn(low1, 1, 1)
    products = mixer_backward(mixer_stored, low1, mixer_weights, channel, place, pump, grads)
    scattered = pump.turn(scatter_rows(products), 0)
    back, gain0 = rms_back(stream0, gains[0], scattered)
    with jax.named_scope("gain_sums"):
        gains_grad = layout.columns_out(jnp.stack([gain0, gain1, gain2, gain3]))
        for axis in ("c", "x", "b") + layout.sums:
            gains_grad = gains_grad + exchange(gains_grad, axis)
    gains_grad = pump.turn(gains_grad, 0)
    pump.flush()
    small = grads["small"]
    with jax.named_scope("last_gather"):
        input_grad = gather_sequence(layout.columns_out((grad1 + back).astype(BF))).astype(F32)
        layer_output = gather_sequence(layout.columns_out(stream4.astype(BF)))

    dp_index = lax.axis_index(layout.high + ("b", "y"))
    select_all, step_all = select_weight.shape[0], step_weight.shape[0]
    select_grad = lax.dynamic_slice_in_dim(small[:select_all], dp_index * select_rows, select_rows, axis=0)
    step_grad = lax.dynamic_slice_in_dim(
        small[select_all : select_all + step_all], dp_index * step_rows, step_rows, axis=0
    )
    rest = small[select_all + step_all :]
    count = conv_taps.shape[0]
    taps_grad, conv_bias_grad, step_bias_grad = rest[:count], rest[count], rest[count + 1]
    decay_grad, skip_grad = rest[count + 2 : count + 2 + states_n], rest[count + 2 + states_n]

    matrix = lambda halves: jnp.concatenate(halves, axis=1).astype(F32)
    pair = lambda low, high: jnp.stack([jnp.concatenate(low, axis=1), jnp.concatenate(high, axis=1)], axis=1).astype(F32)
    parts = lambda halves, count: jnp.stack([h.reshape(here, count, -1) for h in halves], axis=2).astype(F32)
    return (
        layer_output,
        input_grad,
        gains_grad,
        pair([jnp.concatenate(h, axis=1) for h in zip(grads["inner0"], grads["inner1"])], grads["gate"]),
        taps_grad,
        conv_bias_grad,
        select_grad,
        step_grad,
        step_bias_grad,
        decay_grad,
        skip_grad,
        matrix(grads["out"]),
        pair(grads["gate1"], grads["up1"]),
        matrix(grads["down1"]),
        parts(grads["attention_in"], 3).reshape(here, 3, -1),
        matrix(grads["attention_out"]),
        pair(grads["gate2"], grads["up2"]),
        matrix(grads["down2"]),
    )


def solution(mesh):
    n_dp, n_tensor = mesh.devices.shape
    bits = n_dp.bit_length() - 1
    assert n_dp == 1 << bits and bits >= 2 and n_tensor == 4
    high = tuple("a%d" % k for k in range(bits - 2))
    names = high + ("b", "y", "x", "c")
    cube = jax.sharding.Mesh(mesh.devices.reshape((2,) * len(names)), names)
    dp, tensor = high + ("b", "y"), ("x", "c")
    row, both, col = P(dp, None), P(dp, tensor), P(None, tensor)
    three, vec = P(dp, None, tensor), P(tensor)
    return jax.shard_map(
        functools.partial(shards, Layout(high)),
        mesh=cube,
        in_specs=(
            row, row, P(), three, col, vec, both, both, vec, col, vec, both, three, both, three, both, three, both,
        ),
        out_specs=(
            row, row, P(), three, col, vec, both, both, vec, col, vec, both, three, both, three, both, three, both,
        ),
        check_vma=False,
    )
```

time: 1220 us -> 959 us (0.79)
  waiting for transfers between devices: 562 us -> 429 us
  blocking collectives: 66.9 us -> 0 us
  matrix products: 63.3 us -> 122 us
  local copies, waits for them, and re-layouts: 156 us -> 99.5 us
  other arithmetic: 104 us -> 74.1 us
  starting transfers between devices: 194 us -> 176 us
    ppermute x143 -> x147, waiting for transfers between devices: 542 us -> 327 us  [exchange(): return lax.ppermute(value, axis, SWAP)]
    ppermute x16, waiting for transfers between devices: 20.1 us -> 102 us  [exchange_diagonal(): return lax.ppermute(value, ('b', 'x'), ((0, 3), (1, 2), (2, 1), (3, 0)))]
    all_gather x2 -> x0, blocking collectives: 66.9 us -> none  [the longest x1 33.9 us: shards(): lax.all_gather(mixer_select, dp_axes, axis=0, tiled=True)]
    dot_general x13 -> x38, matrix products: 17.9 us -> 55.6 us  [mm_tn(): lax.dot_general(left, right, (((0,), (0,)), ((), ())), preferred_element_...]
    slice x37 -> x25, local copies, waits for them, and re-layouts: 32.2 us -> 6.84 us  [the longest x1 3.39 us: shards(): first = request(['inner0', 'inner1'], [mixer_input[:, 0]])]
    convert_element_type x41 -> x24, other arithmetic: 34.8 us -> 13.5 us  [the longest x4 4.13 us: shards(): matrix = lambda halves: jnp.concatenate(halves, axis=1).astype(F32)]
    ppermute x143 -> x147, starting transfers between devices: 170 us -> 150 us  [exchange(): return lax.ppermute(value, axis, SWAP)]
    reshape x21 -> x17, local copies, waits for them, and re-layouts: 24.4 us -> 5.69 us  [the longest x2 1.44 us: shards(): select_weight = both[:, step_rows:].reshape(-1, conv_out.shape[-1])]
  transfers between devices with their start and end apart: 159 -> 163, of which waited for: 71 -> 74; matrix products, arithmetic and copies ran while one was open for 24% -> 24% of each run, Pallas kernels for 5% -> 4%
where the time goes in v1:
time: 959 us; the launch traced here: 952 us
  waiting for transfers between devices  429 us (45%)
  starting transfers between devices  176 us (18%)
  matrix products  122 us (13%)
  local copies, waits for them, and re-layouts  99.5 us (10%)
  other arithmetic  74.1 us (8%)
  Pallas kernels  46 us (5%)
    ppermute x147, waiting for transfers between devices, exchange(): return lax.ppermute(value, axis, SWAP)  327 us
    ppermute x147, starting transfers between devices, exchange(): return lax.ppermute(value, axis, SWAP)  150 us
    ppermute x16, waiting for transfers between devices, exchange_diagonal(): return lax.ppermute(value, ('b', 'x'), ((0, 3), (1, 2), (2, 1), (3, 0)))  102 us
    dot_general x38, matrix products, mm_tn(): lax.dot_general(left, right, (((0,), (0,)), ((), ())), preferred_element_...  55.6 us
    unnamed x429, local copies, waits for them, and re-layouts  53.1 us
    dot_general x28, matrix products, mm_nt(): lax.dot_general(left, right, (((1,), (1,)), ((), ())), preferred_element_...  38.9 us
    pallas_call x2, Pallas kernels, scan_call(): pl.pallas_call(kernel, grid_spec=pltpu.PrefetchScalarGridSpec(num_scalar_...  38.2 us
    dot_general x15, matrix products, mm(): return jnp.dot(left, right, preferred_element_type=F32)  27.2 us
  transfers between devices with their start and end apart: 163, of which 74 were waited for; matrix products, arithmetic and copies ran while one was open for 24% of the time, Pallas kernels for 4%

profile of v1, /device:TPU:0, one launch (start us, length us, event | category | flops | bytes accessed | tf_op | source)
XLA Modules:
  0.0 951.6 jit_solution(11425061365238403153)
XLA Ops:
  31.8 8.6 collective-permute-done.2
  82.9 7.9 collective-permute-done.15
  132.9 7.5 collective-permute-done.20
  154.2 13.6 %scan_forward.1 = (f32[2,256,512]{2,1,0:T(8,128)S(1)}, f32[2,2,2,64,512]{4,3,2,1,0:T(8,128)S(1)}, f32[2,256,16,512]{3,2,1,0:T(8,128)}) custom-call(s32[2]{0:T(128)S(1)} %pad_add_fusion.place_ref, f32[2,256,512]{2,1,0:T(8,128)S(1)} %get-tuple-element.449.x_ref, f32[2,256,512]{2,1,0:T(8,128)S(1)} %fusion.203.raw_ref, f32[2,2,2,64,512]{4,3,2,1,0:T(8,128)S(1)} %bitcast.278, ...), custom_call_target="tpu_custom_call" | custom-call | flops 83886080 | bytes 16777216 | tf_op jit(solution)/shard_map/scan_forward/pallas_call | solution.py:199
  188.9 9.7 %collective-permute-done.31 = bf16[64,2048]{1,0:T(8,128)(2,1)S(1)} collective-permute-done((bf16[64,2048]{1,0:T(8,128)(2,1)S(1)}, bf16[64,2048]{1,0:T(8,128)(2,1)S(1)}, u32[]{:S(2)}, u32[]{:S(2)}) %collective-permute-start.31) | collective-permute-done | bytes 262176 | tf_op jit(solution)/shard_map/rows_scatter/ppermute | solution.py:349
  233.5 9.8 %collective-permute-done.43 = bf16[512,512]{1,0:T(8,128)(2,1)S(1)} collective-permute-done((bf16[512,512]{1,0:T(8,128)(2,1)S(1)}, bf16[512,512]{1,0:T(8,128)(2,1)S(1)}, u32[]{:S(2)}, u32[]{:S(2)}) %collective-permute-start.43) | collective-permute-done | bytes 524320 | tf_op jit(solution)/shard_map/ppermute | solution.py:345
  256.2 9.8 %collective-permute-done.46 = bf16[512,512]{1,0:T(8,128)(2,1)S(1)} collective-permute-done((bf16[512,512]{1,0:T(8,128)(2,1)S(1)}, bf16[512,512]{1,0:T(8,128)(2,1)S(1)}, u32[]{:S(2)}, u32[]{:S(2)}) %collective-permute-start.46) | collective-permute-done | bytes 524320 | tf_op jit(solution)/shard_map/ppermute | solution.py:345
  277.6 14.4 %collective-permute-done.62 = bf16[256,1536]{1,0:T(8,128)(2,1)S(1)} collective-permute-done((bf16[256,1536]{1,0:T(8,128)(2,1)S(1)}, bf16[256,1536]{1,0:T(8,128)(2,1)S(1)}, u32[]{:S(2)}, u32[]{:S(2)}) %collective-permute-start.62) | collective-permute-done | bytes 786464 | tf_op jit(solution)/shard_map/pack/ppermute | solution.py:345
  302.8 10.4 %collective-permute-done.52 = bf16[64,2048]{1,0:T(8,128)(2,1)S(1)} collective-permute-done((bf16[64,2048]{1,0:T(8,128)(2,1)S(1)}, bf16[64,2048]{1,0:T(8,128)(2,1)S(1)}, u32[]{:S(2)}, u32[]{:S(2)}) %collective-permute-start.52) | collective-permute-done | bytes 262176 | tf_op jit(solution)/shard_map/rows_scatter/ppermute | solution.py:345
  328.2 11.1 %collective-permute-done.58 = bf16[64,2048]{1,0:T(8,128)(2,1)S(1)} collective-permute-done((bf16[64,2048]{1,0:T(8,128)(2,1)S(1)}, bf16[64,2048]{1,0:T(8,128)(2,1)S(1)}, u32[]{:S(2)}, u32[]{:S(2)}) %collective-permute-start.58) | collective-permute-done | bytes 262176 | tf_op jit(solution)/shard_map/rows_gather/ppermute | solution.py:345
  372.4 7.9 collective-permute-done.68
  406.5 7.5 collective-permute-done.73
  418.9 7.3 collective-permute-done.76
  504.1 7.8 collective-permute-done.95
  534.9 17.3 %collective-permute-done.100 = bf16[64,2048]{1,0:T(8,128)(2,1)S(1)} collective-permute-done((bf16[64,2048]{1,0:T(8,128)(2,1)S(1)}, bf16[64,2048]{1,0:T(8,128)(2,1)S(1)}, u32[]{:S(2)}, u32[]{:S(2)}) %collective-permute-start.100) | collective-permute-done | bytes 262176 | tf_op jit(solution)/shard_map/rows_scatter/ppermute | solution.py:349
  577.5 8.1 collective-permute-done.106
  599.9 7.6 collective-permute-done.111
  641.3 21.6 %collective-permute-done.116 = bf16[64,2048]{1,0:T(8,128)(2,1)S(1)} collective-permute-done((bf16[64,2048]{1,0:T(8,128)(2,1)S(1)}, bf16[64,2048]{1,0:T(8,128)(2,1)S(1)}, u32[]{:S(2)}, u32[]{:S(2)}) %collective-permute-start.116) | collective-permute-done | bytes 262176 | tf_op jit(solution)/shard_map/rows_scatter/ppermute | solution.py:349
  737.7 24.6 %scan_backward.1 = (f32[2,2,2,64,512]{4,3,2,1,0:T(8,128)S(1)}, f32[2,256,512]{2,1,0:T(8,128)S(1)}, f32[2,256,512]{2,1,0:T(8,128)S(1)}, f32[2,32,16,128]{3,2,1,0:...) custom-call(s32[2]{0:T(128)S(1)} %pad_add_fusion.place_ref, ...), custom_call_target="tpu_custom_call" | custom-call | flops 251658240 | bytes 16777216 | tf_op jit(solution)/shard_map/scan_backward/pallas_call | solution.py:199
  789.5 21.3 %collective-permute-done.134 = bf16[512,160]{0,1:T(8,128)(2,1)S(1)} collective-permute-done((bf16[512,160]{0,1:T(8,128)(2,1)S(1)}, bf16[512,160]{0,1:T(8,128)(2,1)S(1)}, u32[]{:S(2)}, u32[]{:S(2)}) %collective-permute-start.134) | collective-permute-done | bytes 163872 | tf_op jit(solution)/shard_map/select_return/ppermute | solution.py:345
  815.4 11.1 %collective-permute-done.137 = bf16[512,512]{1,0:T(8,128)(2,1)S(1)} collective-permute-done((bf16[512,512]{1,0:T(8,128)(2,1)S(1)}, bf16[512,512]{1,0:T(8,128)(2,1)S(1)}, u32[]{:S(2)}, u32[]{:S(2)}) %collective-permute-start.137) | collective-permute-done | bytes 524320 | tf_op jit(solution)/shard_map/select_return/ppermute | solution.py:345
  849.3 9.0 collective-permute-done.142
  869.8 9.0 collective-permute-done.144
  910.5 7.8 collective-permute-done.154
  (1121 shorter events, 675.1 us)
Async XLA Ops:
  65.3 31.7 %collective-permute-start.12 = (bf16[512,512]{1,0:T(8,128)(2,1)S(1)}, bf16[512,512]{1,0:T(8,128)(2,1)}, u32[]{:S(2)}, u32[]{:S(2)}) collective-permute-start(bf16[512,512]{1,0:T(8,128)(2,1)S(1)} %pad_maximum_fusion.16), channel_id=1, source_target_pairs={{0,16},{16,0},{1,17},{17,1},{2,18},{18,2},{3,19},{19,3},{4,20},{20... | collective-permute-start | bytes 1572872 | tf_op jit(solution)/shard_map/ppermute | solution.py:345
  65.4 31.6 %collective-permute-start.13 = (bf16[512,512]{1,0:T(8,128)(2,1)S(1)}, bf16[512,512]{1,0:T(8,128)(2,1)}, u32[]{:S(2)}, u32[]{:S(2)}) collective-permute-start(bf16[512,512]{1,0:T(8,128)(2,1)S(1)} %pad_maximum_fusion.16), channel_id=1, source_target_pairs={{0,4},{4,0},{1,5},{5,1},{2,6},{6,2},{3,7},{7,3},{8,12},{12,8},{9,1... | collective-permute-start | bytes 1572872 | tf_op jit(solution)/shard_map/ppermute | solution.py:345
  81.3 39.7 %collective-permute-start.25 = (bf16[256,1536]{1,0:T(8,128)(2,1)}, bf16[256,1536]{1,0:T(8,128)(2,1)}, u32[]{:S(2)}, u32[]{:S(2)}) collective-permute-start(bf16[256,1536]{1,0:T(8,128)(2,1)} %pad_maximum_fusion.13), channel_id=1, source_target_pairs={{0,8},{8,0},{1,9},{9,1},{2,10},{10,2},{3,11},{11,3},{4,12},{12,4},... | collective-permute-start | bytes 2359304 | tf_op jit(solution)/shard_map/pack/ppermute | solution.py:345
  109.4 32.0 %collective-permute-start.21 = (bf16[512,512]{1,0:T(8,128)(2,1)}, bf16[512,512]{1,0:T(8,128)(2,1)}, u32[]{:S(2)}, u32[]{:S(2)}) collective-permute-start(bf16[512,512]{1,0:T(8,128)(2,1)} %collective-permute-done.12), channel_id=1, source_target_pairs={{0,4},{4,0},{1,5},{5,1},{2,6},{6,2},{3,7},{7,3},{8,12},{12,8},{9,1... | collective-permute-start | bytes 1572872 | tf_op jit(solution)/shard_map/ppermute | solution.py:345
  121.0 66.2 %collective-permute-start.38 = (bf16[256,2048]{1,0:T(8,128)(2,1)}, bf16[256,2048]{1,0:T(8,128)(2,1)}, u32[]{:S(2)}, u32[]{:S(2)}) collective-permute-start(bf16[256,2048]{1,0:T(8,128)(2,1)} %pad_maximum_fusion.4), channel_id=1, source_target_pairs={{0,1},{1,0},{2,3},{3,2},{4,5},{5,4},{6,7},{7,6},{8,9},{9,8},{10,11... | collective-permute-start | bytes 3145736 | tf_op jit(solution)/shard_map/rows_gather/ppermute | solution.py:345
  140.4 36.4 %collective-permute-start.47 = (bf16[256,1024]{1,0:T(8,128)(2,1)}, bf16[256,1024]{1,0:T(8,128)(2,1)}, u32[]{:S(2)}, u32[]{:S(2)}) collective-permute-start(bf16[256,1024]{1,0:T(8,128)(2,1)} %pad_maximum_fusion.21), channel_id=1, source_target_pairs={{0,8},{8,0},{1,9},{9,1},{2,10},{10,2},{3,11},{11,3},{4,12},{12,4},... | collective-permute-start | bytes 1572872 | tf_op jit(solution)/shard_map/pack/ppermute | solution.py:345
  524.1 39.5 %collective-permute-start.102 = (bf16[512,512]{1,0:T(8,128)(2,1)S(1)}, bf16[512,512]{1,0:T(8,128)(2,1)S(1)}, u32[]{:S(2)}, u32[]{:S(2)}) collective-permute-start(bf16[512,512]{1,0:T(8,128)(2,1)S(1)} %fusion.27), channel_id=1, source_target_pairs={{0,16},{16,0},{1,17},{17,1},{2,18},{18,2},{3,19},{19,3},{4,20},{20... | collective-permute-start | bytes 1572872 | tf_op jit(solution)/shard_map/ppermute | solution.py:345
  524.9 38.7 %collective-permute-start.103 = (bf16[1024,512]{1,0:T(8,128)(2,1)S(1)}, bf16[1024,512]{1,0:T(8,128)(2,1)S(1)}, u32[]{:S(2)}, u32[]{:S(2)}) collective-permute-start(bf16[1024,512]{1,0:T(8,128)(2,1)S(1)} %copy-done.165), channel_id=1, source_target_pairs={{0,4},{4,0},{1,5},{5,1},{2,6},{6,2},{3,7},{7,3},{8,12},{12,8},{9,1... | collective-permute-start | bytes 3145736 | tf_op jit(solution)/shard_map/ppermute | solution.py:345
  572.9 34.6 %collective-permute-start.110 = (bf16[512,512]{1,0:T(8,128)(2,1)}, bf16[512,512]{1,0:T(8,128)(2,1)}, u32[]{:S(2)}, u32[]{:S(2)}) collective-permute-start(bf16[512,512]{1,0:T(8,128)(2,1)} %fusion.28), channel_id=1, source_target_pairs={{0,16},{16,0},{1,17},{17,1},{2,18},{18,2},{3,19},{19,3},{4,20},{20... | collective-permute-start | bytes 1572872 | tf_op jit(solution)/shard_map/ppermute | solution.py:345
  624.9 50.2 %collective-permute-start.119 = (bf16[512,768]{1,0:T(8,128)(2,1)S(1)}, bf16[512,768]{1,0:T(8,128)(2,1)S(1)}, u32[]{:S(2)}, u32[]{:S(2)}) collective-permute-start(bf16[512,768]{1,0:T(8,128)(2,1)S(1)} %add_convert_fusion.1), channel_id=1, source_target_pairs={{0,16},{16,0},{1,17},{17,1},{2,18},{18,2},{3,19},{19,3},{4,20},{20... | collective-permute-start | bytes 2359304 | tf_op jit(solution)/shard_map/ppermute | solution.py:345
  626.9 48.2 %collective-permute-start.120 = (bf16[1024,512]{1,0:T(8,128)(2,1)S(1)}, bf16[1024,512]{1,0:T(8,128)(2,1)S(1)}, u32[]{:S(2)}, u32[]{:S(2)}) collective-permute-start(bf16[1024,512]{1,0:T(8,128)(2,1)S(1)} %convolution_convert_fusion.9), channel_id=1, source_target_pairs={{0,4},{4,0},{1,5},{5,1},{2,6},{6,2},{3,7},{7,3},{8,12},{12,8},{9,1... | collective-permute-start | bytes 3145736 | tf_op jit(solution)/shard_map/ppermute | solution.py:345
  698.3 64.0 %collective-permute-start.128 = (bf16[1024,512]{1,0:T(8,128)(2,1)}, bf16[1024,512]{1,0:T(8,128)(2,1)}, u32[]{:S(2)}, u32[]{:S(2)}) collective-permute-start(bf16[1024,512]{1,0:T(8,128)(2,1)} %convolution_convert_fusion.7), channel_id=1, source_target_pairs={{0,4},{4,0},{1,5},{5,1},{2,6},{6,2},{3,7},{7,3},{8,12},{12,8},{9,1... | collective-permute-start | bytes 3145736 | tf_op jit(solution)/shard_map/ppermute | solution.py:345
  719.1 43.2 %collective-permute-start.129 = (bf16[256,512]{1,0:T(8,128)(2,1)}, bf16[256,512]{1,0:T(8,128)(2,1)}, u32[]{:S(2)}, u32[]{:S(2)}) collective-permute-start(bf16[256,512]{1,0:T(8,128)(2,1)} %broadcast_select_fusion.40), channel_id=1, source_target_pairs={{0,8},{8,0},{1,9},{9,1},{2,10},{10,2},{3,11},{11,3},{4,12},{12,4},... | collective-permute-start | bytes 786440 | tf_op jit(solution)/shard_map/ppermute | solution.py:345
  719.1 43.3 %collective-permute-start.131 = (bf16[1024,512]{1,0:T(8,128)(2,1)}, bf16[1024,512]{1,0:T(8,128)(2,1)}, u32[]{:S(2)}, u32[]{:S(2)}) collective-permute-start(bf16[1024,512]{1,0:T(8,128)(2,1)} %convolution_convert_fusion.6), channel_id=1, source_target_pairs={{0,4},{4,0},{1,5},{5,1},{2,6},{6,2},{3,7},{7,3},{8,12},{12,8},{9,1... | collective-permute-start | bytes 3145736 | tf_op jit(solution)/shard_map/ppermute | solution.py:345
  723.2 39.2 %collective-permute-start.130 = (bf16[512,512]{1,0:T(8,128)(2,1)}, bf16[512,512]{1,0:T(8,128)(2,1)}, u32[]{:S(2)}, u32[]{:S(2)}) collective-permute-start(bf16[512,512]{1,0:T(8,128)(2,1)} %fusion.30), channel_id=1, source_target_pairs={{0,16},{16,0},{1,17},{17,1},{2,18},{18,2},{3,19},{19,3},{4,20},{20... | collective-permute-start | bytes 1572872 | tf_op jit(solution)/shard_map/ppermute | solution.py:345
  778.7 36.7 %collective-permute-start.135 = (bf16[512,512]{1,0:T(8,128)(2,1)S(1)}, bf16[512,512]{1,0:T(8,128)(2,1)S(1)}, u32[]{:S(2)}, u32[]{:S(2)}) collective-permute-start(bf16[512,512]{1,0:T(8,128)(2,1)S(1)} %fusion.31), channel_id=1, source_target_pairs={{0,16},{16,0},{1,17},{17,1},{2,18},{18,2},{3,19},{19,3},{4,20},{20... | collective-permute-start | bytes 1572872 | tf_op jit(solution)/shard_map/select_return/ppermute | solution.py:345
  784.3 42.2 %collective-permute-start.137 = (bf16[512,512]{1,0:T(8,128)(2,1)S(1)}, bf16[512,512]{1,0:T(8,128)(2,1)S(1)}, u32[]{:S(2)}, u32[]{:S(2)}) collective-permute-start(bf16[512,512]{1,0:T(8,128)(2,1)S(1)} %fusion.32), channel_id=1, source_target_pairs={{0,16},{16,0},{1,17},{17,1},{2,18},{18,2},{3,19},{19,3},{4,20},{20... | collective-permute-start | bytes 1572872 | tf_op jit(solution)/shard_map/select_return/ppermute | solution.py:345
  785.2 41.4 %collective-permute-start.138 = (bf16[1024,512]{1,0:T(8,128)(2,1)S(1)}, bf16[1024,512]{1,0:T(8,128)(2,1)S(1)}, u32[]{:S(2)}, u32[]{:S(2)}) collective-permute-start(bf16[1024,512]{1,0:T(8,128)(2,1)S(1)} %copy-done.176), channel_id=1, source_target_pairs={{0,4},{4,0},{1,5},{5,1},{2,6},{6,2},{3,7},{7,3},{8,12},{12,8},{9,1... | collective-permute-start | bytes 3145736 | tf_op jit(solution)/shard_map/select_return/ppermute | solution.py:345
  836.0 47.1 %collective-permute-start.145 = (bf16[512,512]{1,0:T(8,128)(2,1)}, bf16[512,512]{1,0:T(8,128)(2,1)}, u32[]{:S(2)}, u32[]{:S(2)}) collective-permute-start(bf16[512,512]{1,0:T(8,128)(2,1)} %fusion.33), channel_id=1, source_target_pairs={{0,16},{16,0},{1,17},{17,1},{2,18},{18,2},{3,19},{19,3},{4,20},{20... | collective-permute-start | bytes 1572872 | tf_op jit(solution)/shard_map/ppermute | solution.py:345
  849.0 34.1 %collective-permute-start.146 = (bf16[1024,256]{1,0:T(8,128)(2,1)}, bf16[1024,256]{1,0:T(8,128)(2,1)}, u32[]{:S(2)}, u32[]{:S(2)}) collective-permute-start(bf16[1024,256]{1,0:T(8,128)(2,1)} %convolution_convert_fusion.14), channel_id=1, source_target_pairs={{0,4},{4,0},{1,5},{5,1},{2,6},{6,2},{3,7},{7,3},{8,12},{12,8},{9,1... | collective-permute-start | bytes 1572872 | tf_op jit(solution)/shard_map/ppermute | solution.py:345
  886.3 38.8 %collective-permute-start.149 = (bf16[64,2048]{1,0:T(8,128)(2,1)S(1)}, bf16[64,2048]{1,0:T(8,128)(2,1)}, u32[]{:S(2)}, u32[]{:S(2)}) collective-permute-start(bf16[64,2048]{1,0:T(8,128)(2,1)S(1)} %reshape.504), channel_id=1, source_target_pairs={{0,1},{1,0},{2,3},{3,2},{4,5},{5,4},{6,7},{7,6},{8,9},{9,8},{10,11... | collective-permute-start | bytes 786440 | tf_op jit(solution)/shard_map/last_gather/ppermute | solution.py:345
  889.3 37.7 %collective-permute-start.156 = (bf16[256,512]{1,0:T(8,128)(2,1)S(1)}, bf16[256,512]{1,0:T(8,128)(2,1)S(1)}, u32[]{:S(2)}, u32[]{:S(2)}) collective-permute-start(bf16[256,512]{1,0:T(8,128)(2,1)S(1)} %broadcast_select_fusion.36), channel_id=1, source_target_pairs={{0,8},{8,0},{1,9},{9,1},{2,10},{10,2},{3,11},{11,3},{4,12},{12,4},... | collective-permute-start | bytes 786440 | tf_op jit(solution)/shard_map/ppermute | solution.py:345
  890.8 36.2 %collective-permute-start.157 = (bf16[512,256]{1,0:T(8,128)(2,1)S(1)}, bf16[512,256]{1,0:T(8,128)(2,1)S(1)}, u32[]{:S(2)}, u32[]{:S(2)}) collective-permute-start(bf16[512,256]{1,0:T(8,128)(2,1)S(1)} %fusion.41), channel_id=1, source_target_pairs={{0,16},{16,0},{1,17},{17,1},{2,18},{18,2},{3,19},{19,3},{4,20},{20... | collective-permute-start | bytes 786440 | tf_op jit(solution)/shard_map/ppermute | solution.py:345
  894.5 32.6 %collective-permute-start.158 = (bf16[512,256]{1,0:T(8,128)(2,1)S(1)}, bf16[512,256]{1,0:T(8,128)(2,1)S(1)}, u32[]{:S(2)}, u32[]{:S(2)}) collective-permute-start(bf16[512,256]{1,0:T(8,128)(2,1)S(1)} %fusion.42), channel_id=1, source_target_pairs={{0,16},{16,0},{1,17},{17,1},{2,18},{18,2},{3,19},{19,3},{4,20},{20... | collective-permute-start | bytes 786440 | tf_op jit(solution)/shard_map/ppermute | solution.py:345
  (321 other events, 4613.3 us)

commit v2 on v1

--- a/solution.py
+++ b/solution.py
@@ -157,7 +157,7 @@
         tuple(adj_ref[j] for j in range(blocks)),
         tuple(jnp.zeros((states_n, LANES), jnp.float32) for _ in range(blocks)),
     )
-    adjoint, decay_sum = lax.fori_loop(0, steps // ROWS, chunk, carry, unroll=2)
+    adjoint, decay_sum = lax.fori_loop(0, steps // ROWS, chunk, carry, unroll=4)
     for j in range(blocks):
         adj_ref[j] = adjoint[j]
         ddecay_ref[:, lanes(j)] += rates[j] * decay_sum[j]
@@ -699,6 +699,7 @@
         first = request(["inner0", "inner1"], [mixer_input[:, 0]])
         pump.flush()
     normed0 = gather_rows(tied(rms(stream0, gains[0]), first))
+    normed_first = normed0
     request(["small"], [jnp.concatenate([mixer_step, mixer_select], axis=0)], normed0)
     pump.flush()
     second = request(["gate", "out"], [mixer_input[:, 1], mixer_output], first)
@@ -708,8 +709,8 @@
     normed0 = pump.turn(normed0, 1)
     channel = tuple(mine(v) for v in (conv_taps, conv_bias, step_bias, decay_log, skip_gain))
     inner = jnp.concatenate([mm(normed0, weights["inner0"]), mm(normed0, weights["inner1"])], axis=1)
-    inner = pump.turn(inner, 1)
-    low4 = gather_rows(tied(upstream_rows, inner))
+    low4 = gather_rows(tied(upstream_rows, normed_first))
+    inner = tied(pump.turn(inner, 1), low4)
     inner = in_time(blocks(inner))
     conv_out = jax.nn.silu(conv_total(inner, channel[0], channel[1])).astype(BF)
     select_rows, step_rows = mixer_select.shape[0], mixer_step.shape[0]
@@ -732,7 +733,7 @@
     gated = pump.until(gated, weights, "out")
     mixer_stored = (normed0, inner, gate, conv_out, step_low, raw, sel, mixed, gated, hist)
     mixer_weights = ((weights["inner0"], weights["inner1"]), weights["gate"], weights["out"], select_weight, step_weight)
-    stream1 = tied(pump.turn(stream0 + scatter_rows([(gated, weights["out"])])), low4)
+    stream1 = pump.turn(stream0 + scatter_rows([(gated, weights["out"])]))
     request(
         ["gate2", "up2", "down2"], [second_gate_up, second_down], gated
     )

time: 959 us -> 952 us (level)
  waiting for transfers between devices: 429 us -> 458 us
  matrix products: 122 us -> 102 us
  starting transfers between devices: 176 us -> 162 us
    ppermute x147, waiting for transfers between devices: 327 us -> 361 us  [exchange(): return lax.ppermute(value, axis, SWAP)]
    ppermute x147, starting transfers between devices: 150 us -> 135 us  [exchange(): return lax.ppermute(value, axis, SWAP)]
    dot_general x28, matrix products: 38.9 us -> 26.2 us  [mm_nt(): lax.dot_general(left, right, (((1,), (1,)), ((), ())), preferred_element_...]
    unnamed x429 -> x449, local copies, waits for them, and re-layouts: 53.1 us -> 54.2 us
  transfers between devices with their start and end apart: 163 -> 163, of which waited for: 74 -> 78; matrix products, arithmetic and copies ran while one was open for 24% -> 22% of each run, Pallas kernels for 4% -> 4%
where the time goes in v2:
time: 952 us; the launch traced here: 945 us
  waiting for transfers between devices  458 us (48%)
  starting transfers between devices  162 us (17%)
  local copies, waits for them, and re-layouts  105 us (11%)
  matrix products  102 us (11%)
  other arithmetic  69.2 us (7%)
  Pallas kernels  43.4 us (5%)
    ppermute x147, waiting for transfers between devices, exchange(): return lax.ppermute(value, axis, SWAP)  361 us
    ppermute x147, starting transfers between devices, exchange(): return lax.ppermute(value, axis, SWAP)  135 us
    ppermute x16, waiting for transfers between devices, exchange_diagonal(): return lax.ppermute(value, ('b', 'x'), ((0, 3), (1, 2), (2, 1), (3, 0)))  97.3 us
    dot_general x38, matrix products, mm_tn(): lax.dot_general(left, right, (((0,), (0,)), ((), ())), preferred_element_...  55.7 us
    unnamed x449, local copies, waits for them, and re-layouts  54.2 us
    pallas_call x2, Pallas kernels, scan_call(): pl.pallas_call(kernel, grid_spec=pltpu.PrefetchScalarGridSpec(num_scalar_...  35.5 us
    ppermute x16, starting transfers between devices, exchange_diagonal(): return lax.ppermute(value, ('b', 'x'), ((0, 3), (1, 2), (2, 1), (3, 0)))  26.7 us
    dot_general x28, matrix products, mm_nt(): lax.dot_general(left, right, (((1,), (1,)), ((), ())), preferred_element_...  26.2 us
  transfers between devices with their start and end apart: 163, of which 78 were waited for; matrix products, arithmetic and copies ran while one was open for 22% of the time, Pallas kernels for 4%

profile of v2, /device:TPU:0, one launch (start us, length us, event | category | flops | bytes accessed | tf_op | source)
XLA Modules:
  0.0 944.5 jit_solution(11954233712776157624)
XLA Ops:
  35.2 8.6 collective-permute-done.2
  47.5 7.3 collective-permute-done.5
  87.6 8.9 collective-permute-done.19
  134.4 7.7 collective-permute-done.24
  149.0 13.7 %scan_forward.1 = (f32[2,256,512]{2,1,0:T(8,128)S(1)}, f32[2,2,2,64,512]{4,3,2,1,0:T(8,128)S(1)}, f32[2,256,16,512]{3,2,1,0:T(8,128)}) custom-call(s32[2]{0:T(128)S(1)} %pad_add_fusion.place_ref, f32[2,256,512]{2,1,0:T(8,128)S(1)} %get-tuple-element.449.x_ref, f32[2,256,512]{2,1,0:T(8,128)S(1)} %fusion.203.raw_ref, f32[2,2,2,64,512]{4,3,2,1,0:T(8,128)S(1)} %bitcast.278, ...), custom_call_target="tpu_custom_call" | custom-call | flops 83886080 | bytes 16777216 | tf_op jit(solution)/shard_map/scan_forward/pallas_call | solution.py:199
  183.6 8.9 collective-permute-done.47
  203.2 10.9 %collective-permute-done.34 = bf16[64,2048]{1,0:T(8,128)(2,1)S(1)} collective-permute-done((bf16[64,2048]{1,0:T(8,128)(2,1)S(1)}, bf16[64,2048]{1,0:T(8,128)(2,1)S(1)}, u32[]{:S(2)}, u32[]{:S(2)}) %collective-permute-start.34) | collective-permute-done | bytes 262176 | tf_op jit(solution)/shard_map/rows_scatter/ppermute | solution.py:345
  256.2 15.4 %collective-permute-done.46 = bf16[512,512]{1,0:T(8,128)(2,1)S(1)} collective-permute-done((bf16[512,512]{1,0:T(8,128)(2,1)S(1)}, bf16[512,512]{1,0:T(8,128)(2,1)S(1)}, u32[]{:S(2)}, u32[]{:S(2)}) %collective-permute-start.46) | collective-permute-done | bytes 524320 | tf_op jit(solution)/shard_map/ppermute | solution.py:345
  277.7 17.3 %collective-permute-done.62 = bf16[256,1536]{1,0:T(8,128)(2,1)S(1)} collective-permute-done((bf16[256,1536]{1,0:T(8,128)(2,1)S(1)}, bf16[256,1536]{1,0:T(8,128)(2,1)S(1)}, u32[]{:S(2)}, u32[]{:S(2)}) %collective-permute-start.62) | collective-permute-done | bytes 786464 | tf_op jit(solution)/shard_map/pack/ppermute | solution.py:345
  305.6 10.2 %collective-permute-done.52 = bf16[64,2048]{1,0:T(8,128)(2,1)S(1)} collective-permute-done((bf16[64,2048]{1,0:T(8,128)(2,1)S(1)}, bf16[64,2048]{1,0:T(8,128)(2,1)S(1)}, u32[]{:S(2)}, u32[]{:S(2)}) %collective-permute-start.52) | collective-permute-done | bytes 262176 | tf_op jit(solution)/shard_map/rows_scatter/ppermute | solution.py:345
  329.1 10.8 %collective-permute-done.58 = bf16[64,2048]{1,0:T(8,128)(2,1)S(1)} collective-permute-done((bf16[64,2048]{1,0:T(8,128)(2,1)S(1)}, bf16[64,2048]{1,0:T(8,128)(2,1)S(1)}, u32[]{:S(2)}, u32[]{:S(2)}) %collective-permute-start.58) | collective-permute-done | bytes 262176 | tf_op jit(solution)/shard_map/rows_gather/ppermute | solution.py:345
  373.5 12.0 %collective-permute-done.68 = bf16[64,2048]{1,0:T(8,128)(2,1)} collective-permute-done((bf16[64,2048]{1,0:T(8,128)(2,1)S(1)}, bf16[64,2048]{1,0:T(8,128)(2,1)}, u32[]{:S(2)}, u32[]{:S(2)}) %collective-permute-start.68) | collective-permute-done | bytes 262176 | tf_op jit(solution)/shard_map/rows_scatter/ppermute | solution.py:349
  535.9 17.3 %collective-permute-done.100 = bf16[64,2048]{1,0:T(8,128)(2,1)S(1)} collective-permute-done((bf16[64,2048]{1,0:T(8,128)(2,1)S(1)}, bf16[64,2048]{1,0:T(8,128)(2,1)S(1)}, u32[]{:S(2)}, u32[]{:S(2)}) %collective-permute-start.100) | collective-permute-done | bytes 262176 | tf_op jit(solution)/shard_map/rows_scatter/ppermute | solution.py:349
  576.4 9.7 %collective-permute-done.106 = bf16[64,2048]{1,0:T(8,128)(2,1)} collective-permute-done((bf16[64,2048]{1,0:T(8,128)(2,1)S(1)}, bf16[64,2048]{1,0:T(8,128)(2,1)}, u32[]{:S(2)}, u32[]{:S(2)}) %collective-permute-start.106) | collective-permute-done | bytes 262176 | tf_op jit(solution)/shard_map/rows_gather/ppermute | solution.py:345
  596.3 9.7 %collective-permute-done.111 = bf16[512,256]{1,0:T(8,128)(2,1)S(1)} collective-permute-done((bf16[512,256]{1,0:T(8,128)(2,1)S(1)}, bf16[512,256]{1,0:T(8,128)(2,1)S(1)}, u32[]{:S(2)}, u32[]{:S(2)}) %collective-permute-start.111) | collective-permute-done | bytes 262176 | tf_op jit(solution)/shard_map/ppermute | solution.py:345
  633.1 12.3 %collective-permute-done.116 = bf16[64,2048]{1,0:T(8,128)(2,1)S(1)} collective-permute-done((bf16[64,2048]{1,0:T(8,128)(2,1)S(1)}, bf16[64,2048]{1,0:T(8,128)(2,1)S(1)}, u32[]{:S(2)}, u32[]{:S(2)}) %collective-permute-start.116) | collective-permute-done | bytes 262176 | tf_op jit(solution)/shard_map/rows_scatter/ppermute | solution.py:349
  648.7 11.6 %collective-permute-done.115 = bf16[64,2048]{1,0:T(8,128)(2,1)S(1)} collective-permute-done((bf16[64,2048]{1,0:T(8,128)(2,1)S(1)}, bf16[64,2048]{1,0:T(8,128)(2,1)S(1)}, u32[]{:S(2)}, u32[]{:S(2)}) %collective-permute-start.115) | collective-permute-done | bytes 262176 | tf_op jit(solution)/shard_map/rows_scatter/ppermute | solution.py:345
  683.3 7.5 collective-permute-done.122
  729.4 21.9 %scan_backward.1 = (f32[2,2,2,64,512]{4,3,2,1,0:T(8,128)S(1)}, f32[2,256,512]{2,1,0:T(8,128)S(1)}, f32[2,256,512]{2,1,0:T(8,128)S(1)}, f32[2,32,16,128]{3,2,1,0:...) custom-call(s32[2]{0:T(128)S(1)} %pad_add_fusion.place_ref, ...), custom_call_target="tpu_custom_call" | custom-call | flops 251658240 | bytes 16777216 | tf_op jit(solution)/shard_map/scan_backward/pallas_call | solution.py:199
  781.0 21.2 %collective-permute-done.134 = bf16[512,160]{0,1:T(8,128)(2,1)S(1)} collective-permute-done((bf16[512,160]{0,1:T(8,128)(2,1)S(1)}, bf16[512,160]{0,1:T(8,128)(2,1)S(1)}, u32[]{:S(2)}, u32[]{:S(2)}) %collective-permute-start.134) | collective-permute-done | bytes 163872 | tf_op jit(solution)/shard_map/select_return/ppermute | solution.py:345
  806.8 11.2 %collective-permute-done.137 = bf16[512,512]{1,0:T(8,128)(2,1)S(1)} collective-permute-done((bf16[512,512]{1,0:T(8,128)(2,1)S(1)}, bf16[512,512]{1,0:T(8,128)(2,1)S(1)}, u32[]{:S(2)}, u32[]{:S(2)}) %collective-permute-start.137) | collective-permute-done | bytes 524320 | tf_op jit(solution)/shard_map/select_return/ppermute | solution.py:345
  842.9 12.8 %collective-permute-done.142 = bf16[64,2048]{1,0:T(8,128)(2,1)S(1)} collective-permute-done((bf16[64,2048]{1,0:T(8,128)(2,1)S(1)}, bf16[64,2048]{1,0:T(8,128)(2,1)S(1)}, u32[]{:S(2)}, u32[]{:S(2)}) %collective-permute-start.142) | collective-permute-done | bytes 262176 | tf_op jit(solution)/shard_map/rows_scatter/ppermute | solution.py:349
  863.4 8.4 collective-permute-done.144
  902.9 7.9 collective-permute-done.154
  (1141 shorter events, 655.8 us)
Async XLA Ops:
  69.5 31.9 %collective-permute-start.14 = (bf16[64,2048]{1,0:T(8,128)(2,1)S(1)}, bf16[64,2048]{1,0:T(8,128)(2,1)}, u32[]{:S(2)}, u32[]{:S(2)}) collective-permute-start(bf16[64,2048]{1,0:T(8,128)(2,1)S(1)} %reshape.475), channel_id=1, source_target_pairs={{0,2},{2,0},{1,3},{3,1},{4,6},{6,4},{5,7},{7,5},{8,10},{10,8},{9,1... | collective-permute-start | bytes 786440 | tf_op jit(solution)/shard_map/rows_gather/ppermute | solution.py:345
  72.0 29.8 %collective-permute-start.15 = (bf16[64,2048]{1,0:T(8,128)(2,1)S(1)}, bf16[64,2048]{1,0:T(8,128)(2,1)}, u32[]{:S(2)}, u32[]{:S(2)}) collective-permute-start(bf16[64,2048]{1,0:T(8,128)(2,1)S(1)} %reshape.475), channel_id=1, source_target_pairs={{0,8},{8,0},{1,9},{9,1},{2,10},{10,2},{3,11},{11,3},{4,12},{12,4},... | collective-permute-start | bytes 786440 | tf_op jit(solution)/shard_map/rows_gather/ppermute | solution.py:345
  524.8 38.3 %collective-permute-start.102 = (bf16[512,512]{1,0:T(8,128)(2,1)S(1)}, bf16[512,512]{1,0:T(8,128)(2,1)S(1)}, u32[]{:S(2)}, u32[]{:S(2)}) collective-permute-start(bf16[512,512]{1,0:T(8,128)(2,1)S(1)} %fusion.27), channel_id=1, source_target_pairs={{0,16},{16,0},{1,17},{17,1},{2,18},{18,2},{3,19},{19,3},{4,20},{20... | collective-permute-start | bytes 1572872 | tf_op jit(solution)/shard_map/ppermute | solution.py:345
  525.7 37.5 %collective-permute-start.103 = (bf16[1024,512]{1,0:T(8,128)(2,1)S(1)}, bf16[1024,512]{1,0:T(8,128)(2,1)S(1)}, u32[]{:S(2)}, u32[]{:S(2)}) collective-permute-start(bf16[1024,512]{1,0:T(8,128)(2,1)S(1)} %copy-done.175), channel_id=1, source_target_pairs={{0,4},{4,0},{1,5},{5,1},{2,6},{6,2},{3,7},{7,3},{8,12},{12,8},{9,1... | collective-permute-start | bytes 3145736 | tf_op jit(solution)/shard_map/ppermute | solution.py:345
  571.8 34.2 %collective-permute-start.110 = (bf16[512,512]{1,0:T(8,128)(2,1)}, bf16[512,512]{1,0:T(8,128)(2,1)}, u32[]{:S(2)}, u32[]{:S(2)}) collective-permute-start(bf16[512,512]{1,0:T(8,128)(2,1)} %fusion.28), channel_id=1, source_target_pairs={{0,16},{16,0},{1,17},{17,1},{2,18},{18,2},{3,19},{19,3},{4,20},{20... | collective-permute-start | bytes 1572872 | tf_op jit(solution)/shard_map/ppermute | solution.py:345
  575.8 30.3 %collective-permute-start.111 = (bf16[512,256]{1,0:T(8,128)(2,1)S(1)}, bf16[512,256]{1,0:T(8,128)(2,1)S(1)}, u32[]{:S(2)}, u32[]{:S(2)}) collective-permute-start(bf16[512,256]{1,0:T(8,128)(2,1)S(1)} %fusion.40), channel_id=1, source_target_pairs={{0,16},{16,0},{1,17},{17,1},{2,18},{18,2},{3,19},{19,3},{4,20},{20... | collective-permute-start | bytes 786440 | tf_op jit(solution)/shard_map/ppermute | solution.py:345
  619.6 47.8 %collective-permute-start.119 = (bf16[512,768]{1,0:T(8,128)(2,1)S(1)}, bf16[512,768]{1,0:T(8,128)(2,1)S(1)}, u32[]{:S(2)}, u32[]{:S(2)}) collective-permute-start(bf16[512,768]{1,0:T(8,128)(2,1)S(1)} %add_convert_fusion.1), channel_id=1, source_target_pairs={{0,16},{16,0},{1,17},{17,1},{2,18},{18,2},{3,19},{19,3},{4,20},{20... | collective-permute-start | bytes 2359304 | tf_op jit(solution)/shard_map/ppermute | solution.py:345
  621.8 46.2 %collective-permute-start.120 = (bf16[1024,512]{1,0:T(8,128)(2,1)S(1)}, bf16[1024,512]{1,0:T(8,128)(2,1)S(1)}, u32[]{:S(2)}, u32[]{:S(2)}) collective-permute-start(bf16[1024,512]{1,0:T(8,128)(2,1)S(1)} %convolution_convert_fusion.9), channel_id=1, source_target_pairs={{0,4},{4,0},{1,5},{5,1},{2,6},{6,2},{3,7},{7,3},{8,12},{12,8},{9,1... | collective-permute-start | bytes 3145736 | tf_op jit(solution)/shard_map/ppermute | solution.py:345
  630.0 30.2 %collective-permute-start.115 = (bf16[64,2048]{1,0:T(8,128)(2,1)S(1)}, bf16[64,2048]{1,0:T(8,128)(2,1)S(1)}, u32[]{:S(2)}, u32[]{:S(2)}) collective-permute-start(bf16[64,2048]{1,0:T(8,128)(2,1)S(1)} %get-tuple-element.490), channel_id=1, source_target_pairs={{0,8},{8,0},{1,9},{9,1},{2,10},{10,2},{3,11},{11,3},{4,12},{12,4},... | collective-permute-start | bytes 786440 | tf_op jit(solution)/shard_map/rows_scatter/ppermute | solution.py:345
  674.0 30.4 %collective-permute-start.125 = (bf16[256,768]{1,0:T(8,128)(2,1)}, bf16[256,768]{1,0:T(8,128)(2,1)}, u32[]{:S(2)}, u32[]{:S(2)}) collective-permute-start(bf16[256,768]{1,0:T(8,128)(2,1)} %broadcast_select_fusion.11), channel_id=1, source_target_pairs={{0,8},{8,0},{1,9},{9,1},{2,10},{10,2},{3,11},{11,3},{4,12},{12,4},... | collective-permute-start | bytes 1179656 | tf_op jit(solution)/shard_map/ppermute | solution.py:345
  690.8 60.4 %collective-permute-start.128 = (bf16[1024,512]{1,0:T(8,128)(2,1)}, bf16[1024,512]{1,0:T(8,128)(2,1)}, u32[]{:S(2)}, u32[]{:S(2)}) collective-permute-start(bf16[1024,512]{1,0:T(8,128)(2,1)} %convolution_convert_fusion.7), channel_id=1, source_target_pairs={{0,4},{4,0},{1,5},{5,1},{2,6},{6,2},{3,7},{7,3},{8,12},{12,8},{9,1... | collective-permute-start | bytes 3145736 | tf_op jit(solution)/shard_map/ppermute | solution.py:345
  711.2 40.1 %collective-permute-start.129 = (bf16[256,512]{1,0:T(8,128)(2,1)}, bf16[256,512]{1,0:T(8,128)(2,1)}, u32[]{:S(2)}, u32[]{:S(2)}) collective-permute-start(bf16[256,512]{1,0:T(8,128)(2,1)} %broadcast_select_fusion.40), channel_id=1, source_target_pairs={{0,8},{8,0},{1,9},{9,1},{2,10},{10,2},{3,11},{11,3},{4,12},{12,4},... | collective-permute-start | bytes 786440 | tf_op jit(solution)/shard_map/ppermute | solution.py:345
  711.2 40.1 %collective-permute-start.131 = (bf16[1024,512]{1,0:T(8,128)(2,1)}, bf16[1024,512]{1,0:T(8,128)(2,1)}, u32[]{:S(2)}, u32[]{:S(2)}) collective-permute-start(bf16[1024,512]{1,0:T(8,128)(2,1)} %convolution_convert_fusion.6), channel_id=1, source_target_pairs={{0,4},{4,0},{1,5},{5,1},{2,6},{6,2},{3,7},{7,3},{8,12},{12,8},{9,1... | collective-permute-start | bytes 3145736 | tf_op jit(solution)/shard_map/ppermute | solution.py:345
  714.7 36.6 %collective-permute-start.130 = (bf16[512,512]{1,0:T(8,128)(2,1)}, bf16[512,512]{1,0:T(8,128)(2,1)}, u32[]{:S(2)}, u32[]{:S(2)}) collective-permute-start(bf16[512,512]{1,0:T(8,128)(2,1)} %fusion.30), channel_id=1, source_target_pairs={{0,16},{16,0},{1,17},{17,1},{2,18},{18,2},{3,19},{19,3},{4,20},{20... | collective-permute-start | bytes 1572872 | tf_op jit(solution)/shard_map/ppermute | solution.py:345
  769.9 36.9 %collective-permute-start.135 = (bf16[512,512]{1,0:T(8,128)(2,1)S(1)}, bf16[512,512]{1,0:T(8,128)(2,1)S(1)}, u32[]{:S(2)}, u32[]{:S(2)}) collective-permute-start(bf16[512,512]{1,0:T(8,128)(2,1)S(1)} %fusion.31), channel_id=1, source_target_pairs={{0,16},{16,0},{1,17},{17,1},{2,18},{18,2},{3,19},{19,3},{4,20},{20... | collective-permute-start | bytes 1572872 | tf_op jit(solution)/shard_map/select_return/ppermute | solution.py:345
  772.0 30.3 %collective-permute-start.136 = (bf16[256,512]{1,0:T(8,128)(2,1)S(1)}, bf16[256,512]{1,0:T(8,128)(2,1)S(1)}, u32[]{:S(2)}, u32[]{:S(2)}) collective-permute-start(bf16[256,512]{1,0:T(8,128)(2,1)S(1)} %broadcast_select_fusion.39), channel_id=1, source_target_pairs={{0,8},{8,0},{1,9},{9,1},{2,10},{10,2},{3,11},{11,3},{4,12},{12,4},... | collective-permute-start | bytes 786440 | tf_op jit(solution)/shard_map/select_return/ppermute | solution.py:345
  775.4 42.6 %collective-permute-start.137 = (bf16[512,512]{1,0:T(8,128)(2,1)S(1)}, bf16[512,512]{1,0:T(8,128)(2,1)S(1)}, u32[]{:S(2)}, u32[]{:S(2)}) collective-permute-start(bf16[512,512]{1,0:T(8,128)(2,1)S(1)} %fusion.32), channel_id=1, source_target_pairs={{0,16},{16,0},{1,17},{17,1},{2,18},{18,2},{3,19},{19,3},{4,20},{20... | collective-permute-start | bytes 1572872 | tf_op jit(solution)/shard_map/select_return/ppermute | solution.py:345
  776.3 41.7 %collective-permute-start.138 = (bf16[1024,512]{1,0:T(8,128)(2,1)S(1)}, bf16[1024,512]{1,0:T(8,128)(2,1)S(1)}, u32[]{:S(2)}, u32[]{:S(2)}) collective-permute-start(bf16[1024,512]{1,0:T(8,128)(2,1)S(1)} %copy-done.186), channel_id=1, source_target_pairs={{0,4},{4,0},{1,5},{5,1},{2,6},{6,2},{3,7},{7,3},{8,12},{12,8},{9,1... | collective-permute-start | bytes 3145736 | tf_op jit(solution)/shard_map/select_return/ppermute | solution.py:345
  827.7 47.9 %collective-permute-start.145 = (bf16[512,512]{1,0:T(8,128)(2,1)}, bf16[512,512]{1,0:T(8,128)(2,1)}, u32[]{:S(2)}, u32[]{:S(2)}) collective-permute-start(bf16[512,512]{1,0:T(8,128)(2,1)} %fusion.33), channel_id=1, source_target_pairs={{0,16},{16,0},{1,17},{17,1},{2,18},{18,2},{3,19},{19,3},{4,20},{20... | collective-permute-start | bytes 1572872 | tf_op jit(solution)/shard_map/ppermute | solution.py:345
  842.0 33.6 %collective-permute-start.146 = (bf16[1024,256]{1,0:T(8,128)(2,1)}, bf16[1024,256]{1,0:T(8,128)(2,1)}, u32[]{:S(2)}, u32[]{:S(2)}) collective-permute-start(bf16[1024,256]{1,0:T(8,128)(2,1)} %convolution_convert_fusion.14), channel_id=1, source_target_pairs={{0,4},{4,0},{1,5},{5,1},{2,6},{6,2},{3,7},{7,3},{8,12},{12,8},{9,1... | collective-permute-start | bytes 1572872 | tf_op jit(solution)/shard_map/ppermute | solution.py:345
  878.8 38.7 %collective-permute-start.149 = (bf16[64,2048]{1,0:T(8,128)(2,1)S(1)}, bf16[64,2048]{1,0:T(8,128)(2,1)}, u32[]{:S(2)}, u32[]{:S(2)}) collective-permute-start(bf16[64,2048]{1,0:T(8,128)(2,1)S(1)} %reshape.504), channel_id=1, source_target_pairs={{0,1},{1,0},{2,3},{3,2},{4,5},{5,4},{6,7},{7,6},{8,9},{9,8},{10,11... | collective-permute-start | bytes 786440 | tf_op jit(solution)/shard_map/last_gather/ppermute | solution.py:345
  881.8 37.6 %collective-permute-start.156 = (bf16[256,512]{1,0:T(8,128)(2,1)S(1)}, bf16[256,512]{1,0:T(8,128)(2,1)S(1)}, u32[]{:S(2)}, u32[]{:S(2)}) collective-permute-start(bf16[256,512]{1,0:T(8,128)(2,1)S(1)} %broadcast_select_fusion.36), channel_id=1, source_target_pairs={{0,8},{8,0},{1,9},{9,1},{2,10},{10,2},{3,11},{11,3},{4,12},{12,4},... | collective-permute-start | bytes 786440 | tf_op jit(solution)/shard_map/ppermute | solution.py:345
  883.3 36.1 %collective-permute-start.157 = (bf16[512,256]{1,0:T(8,128)(2,1)S(1)}, bf16[512,256]{1,0:T(8,128)(2,1)S(1)}, u32[]{:S(2)}, u32[]{:S(2)}) collective-permute-start(bf16[512,256]{1,0:T(8,128)(2,1)S(1)} %fusion.41), channel_id=1, source_target_pairs={{0,16},{16,0},{1,17},{17,1},{2,18},{18,2},{3,19},{19,3},{4,20},{20... | collective-permute-start | bytes 786440 | tf_op jit(solution)/shard_map/ppermute | solution.py:345
  886.8 32.5 %collective-permute-start.158 = (bf16[512,256]{1,0:T(8,128)(2,1)S(1)}, bf16[512,256]{1,0:T(8,128)(2,1)S(1)}, u32[]{:S(2)}, u32[]{:S(2)}) collective-permute-start(bf16[512,256]{1,0:T(8,128)(2,1)S(1)} %fusion.42), channel_id=1, source_target_pairs={{0,16},{16,0},{1,17},{17,1},{2,18},{18,2},{3,19},{19,3},{4,20},{20... | collective-permute-start | bytes 786440 | tf_op jit(solution)/shard_map/ppermute | solution.py:345
  (331 other events, 4649.3 us)
